TPU v7x, 32 devices: a whole 2x2x4 slice. The times are simulated.
32 devices in a mesh: lon: 4 (over y, core), batch: 8 (over z, x).
Axes of the slice: x: 2, y: 2, z: 4, core: 2. Of those that a mesh axis runs over, the one named last changes fastest.
Arguments:
- fields: float32 [8, 32, 64, 5], P('batch', None, 'lon'), may hold values from -6 to 6
- velocity: float32 [8, 32, 64, 10], P('batch', None, 'lon'), may hold values from -3 to 3
- context: float32 [8, 32, 64, 75], P('batch', None, 'lon'), may hold values from -6 to 6
- masks: int32 [8, 32, 64], P('batch', None, 'lon'), may hold values from 0 to 1, as said below
- window: int32 [32, 64, 8], P(None, 'lon'), may hold values from 0 to 95
- lift_weight: float32 [3, 3, 100, 128], replicated, may hold values from -0.1875 to 0.1875
- lift_bias: float32 [128], replicated, may hold values from -3 to 3
- norm_gain: float32 [2, 128], replicated, may hold values from 0.5 to 1.5
- norm_shift: float32 [2, 128], replicated, may hold values from -3 to 3
- conv_weight: float32 [2, 3, 3, 128, 128], replicated, may hold values from -0.1875 to 0.1875
- attn_qkv: float32 [128, 384], replicated, may hold values from -0.5 to 0.5
- attn_out: float32 [128, 128], replicated, may hold values from -1 to 1
- head_weight: float32 [128, 10], replicated, may hold values from -0.5 to 0.5
- head_bias: float32 [10], replicated, may hold values from -3 to 3
- cot_fields: float32 [8, 32, 64, 5], P('batch', None, 'lon'), may hold values from -6 to 6
- cot_velocity: float32 [8, 32, 64, 10], P('batch', None, 'lon'), may hold values from -6 to 6
Outputs:
- new_fields: float32 [8, 32, 64, 5], P('batch', None, 'lon')
- new_velocity: float32 [8, 32, 64, 10], P('batch', None, 'lon')
- grad_fields: float32 [8, 32, 64, 5], P('batch', None, 'lon')
- grad_velocity: float32 [8, 32, 64, 10], P('batch', None, 'lon')
- grad_lift_weight: float32 [3, 3, 100, 128], replicated
- grad_lift_bias: float32 [128], replicated
- grad_norm_gain: float32 [2, 128], replicated
- grad_norm_shift: float32 [2, 128], replicated
- grad_conv_weight: float32 [2, 3, 3, 128, 128], replicated
- grad_attn_qkv: float32 [128, 384], replicated
- grad_attn_out: float32 [128, 128], replicated
- grad_head_weight: float32 [128, 10], replicated
- grad_head_bias: float32 [10], replicated
Inputs may be any that keep to these rules, and one draw needn't show every extreme that they name: `masks`: 1 marks a pixel counted in the statistics; latitude row 16 is counted in every sample and column. `window`: entry k names the key at latitude k % 32 in the column k // 32 - 1 places east of the query's, around the longitude circle.
All inputs are finite; a program needn't handle non-finite values.
Results may differ from a plain program's by a relative error of at most 0.0003.
Values sent between devices are 32-bit elements; how exact they have to be, the bound alone decides.
A program may use at most 320 MiB of HBM per device.

v0:
```python
from functools import partial

import jax
import jax.numpy as jnp
from jax import lax
from jax.sharding import PartitionSpec as P

HEADS = 4


highest = lax.Precision.HIGHEST
epsilon = 1e-05
step_size = 0.25


def padded_2(block, sides, width):
    for axis, dim in sides:
        count = lax.axis_size(axis)
        forward = [(i, i + 1) for i in range(count - 1)]
        forward.append((count - 1, 0))
        backward = [(target, source) for source, target in forward]
        low = lax.ppermute(
            lax.slice_in_dim(block, block.shape[dim] - width, None, axis=dim), axis, forward
        )
        high = lax.ppermute(lax.slice_in_dim(block, 0, width, axis=dim), axis, backward)
        block = jnp.concatenate([low, block, high], axis=dim)
    return block


def lon_pad(values):
    return padded_2(values, (("lon", 2),), 1)


def lon_unpad(grad_padded):
    edge_cols = jnp.concatenate([grad_padded[:, :, :1], grad_padded[:, :, -1:]], axis=2)
    beside_all = padded_2(edge_cols, (("lon", 2),), 1)
    interior = grad_padded[:, :, 1:-1]
    interior = interior.at[:, :, 0].add(beside_all[:, :, 0])
    return interior.at[:, :, -1].add(beside_all[:, :, 3])


def flux_stack(fields, velocity):
    count_var = fields.shape[-1]
    return jnp.concatenate(
        [fields, fields * velocity[..., :count_var], fields * velocity[..., count_var:]], axis=-1
    )


def state_terms(padded, velocity, context):
    count_var = velocity.shape[-1] // 2
    framed = jnp.pad(padded, ((0, 0), (1, 1), (0, 0), (0, 0)))
    centre = framed[:, 1:-1, 1:-1]
    lat_diff = 0.5 * (framed[:, 2:, 1:-1] - framed[:, :-2, 1:-1])
    lon_diff = 0.5 * (framed[:, 1:-1, 2:] - framed[:, 1:-1, :-2])
    tendency = -(lat_diff[..., count_var : 2 * count_var] + lon_diff[..., 2 * count_var :])
    inputs = jnp.concatenate(
        [
            centre[..., :count_var],
            lat_diff[..., :count_var],
            lon_diff[..., :count_var],
            velocity,
            context,
        ],
        axis=-1,
    )
    return (inputs, tendency)


def conv_same(padded, kernel):
    return lax.conv_general_dilated(
        padded,
        kernel,
        (1, 1),
        ((1, 1), (0, 0)),
        dimension_numbers=("NHWC", "HWIO", "NHWC"),
        precision=highest,
    )


def lift_layer(padded, kernel, bias_vec):
    return conv_same(padded, kernel) + bias_vec


def norm_act(hidden, first_sum, second_sum, gain_row, shift_row, total_count):
    average = first_sum / total_count
    spread = second_sum / total_count - average * average
    scaled = (hidden - average) * lax.rsqrt(spread + epsilon) * gain_row + shift_row
    return jax.nn.gelu(scaled, approximate=False)


def project_keys(hidden, qkv_weight):
    mixing = jnp.einsum("abcd,de->abce", hidden, qkv_weight, precision=highest)
    channels = hidden.shape[-1]
    return (mixing[..., :channels], mixing[..., channels:])


def attend(queries, keyval_padded, out_weight, window_local):
    samples, lat_count, lon_count, channels = queries.shape
    keys_count = window_local.shape[-1]
    padded_width = lon_count + 2
    head_size = channels // HEADS
    column = lax.broadcasted_iota(jnp.int32, window_local.shape, 1)
    flat_index = window_local % lat_count * padded_width + column + window_local // lat_count
    flat_pairs = keyval_padded.reshape(samples, lat_count * padded_width, 2 * channels)
    picked = jnp.take(flat_pairs, flat_index.reshape(-1), axis=1)
    picked = picked.reshape(samples, lat_count, lon_count, keys_count, 2, HEADS, head_size)
    heads_query = queries.reshape(samples, lat_count, lon_count, HEADS, head_size)
    scores = jnp.einsum(
        "abchd,abcwhd->abchw", heads_query, picked[..., 0, :, :], precision=highest
    ) * head_size ** (-0.5)
    weights = jax.nn.softmax(scores, axis=-1)
    blended = jnp.einsum("abchw,abcwhd->abchd", weights, picked[..., 1, :, :], precision=highest)
    return jnp.einsum(
        "abce,ef->abcf",
        blended.reshape(samples, lat_count, lon_count, channels),
        out_weight,
        precision=highest,
    )


def head_layer(hidden, head_weight, bias_vec):
    return jnp.einsum("abcd,de->abce", hidden, head_weight, precision=highest) + bias_vec


def velocity_field(fields, velocity, context, weight_mask, window_local, params):
    (
        lift_weight,
        lift_bias,
        norm_gain,
        norm_shift,
        conv_weight,
        attn_qkv,
        attn_out,
        head_weight,
        head_bias,
    ) = params
    stacked, pull_stack = jax.vjp(flux_stack, fields, velocity)
    (inputs, tendency), pull_terms = jax.vjp(
        partial(state_terms, context=context), lon_pad(stacked), velocity
    )
    hidden, pull_lift = jax.vjp(lift_layer, lon_pad(inputs), lift_weight, lift_bias)
    blocks = []
    for block_index in range(norm_gain.shape[0]):
        weighted = hidden * weight_mask[..., None]
        first_sum, second_sum, total_count = lax.psum(
            (
                jnp.sum(weighted, axis=(0, 1, 2)),
                jnp.sum(weighted * hidden, axis=(0, 1, 2)),
                jnp.sum(weight_mask),
            ),
            ("lon", "batch"),
        )
        activity, pull_act = jax.vjp(
            partial(norm_act, total_count=total_count),
            hidden,
            first_sum,
            second_sum,
            norm_gain[block_index],
            norm_shift[block_index],
        )
        update, pull_conv = jax.vjp(conv_same, lon_pad(activity), conv_weight[block_index])
        blocks.append((hidden, pull_act, pull_conv))
        hidden = hidden + update
    (queries, keyval), pull_proj = jax.vjp(project_keys, hidden, attn_qkv)
    update, pull_attend = jax.vjp(
        partial(attend, window_local=window_local), queries, lon_pad(keyval), attn_out
    )
    hidden = hidden + update
    acceleration, pull_head = jax.vjp(head_layer, hidden, head_weight, head_bias)
    record = (
        pull_stack,
        pull_terms,
        pull_lift,
        blocks,
        pull_proj,
        pull_attend,
        pull_head,
        stacked.shape[-1],
    )
    return ((tendency, acceleration), record)


def velocity_back(record, weight_mask, grad_tendency, grad_accel):
    pull_stack, pull_terms, pull_lift, blocks, pull_proj, pull_attend, pull_head, count_stack = (
        record
    )
    grad_hidden, grad_head_w, grad_head_b = pull_head(grad_accel)
    grad_query, grad_kv_padded, grad_out = pull_attend(grad_hidden)
    grad_from_proj, grad_qkv = pull_proj((grad_query, lon_unpad(grad_kv_padded)))
    grad_hidden = grad_hidden + grad_from_proj
    gains_list, shifts_list, kernels_list = ([], [], [])
    for hidden, pull_act, pull_conv in reversed(blocks):
        grad_act_padded, grad_kernel = pull_conv(grad_hidden)
        grad_direct, grad_first, grad_second, grad_gain, grad_shift = pull_act(
            lon_unpad(grad_act_padded)
        )
        total_first, total_second = lax.psum((grad_first, grad_second), ("lon", "batch"))
        grad_hidden = (
            grad_hidden
            + grad_direct
            + weight_mask[..., None] * (total_first + 2.0 * hidden * total_second)
        )
        gains_list.append(grad_gain)
        shifts_list.append(grad_shift)
        kernels_list.append(grad_kernel)
    grad_in_padded, grad_lift_w, grad_lift_b = pull_lift(grad_hidden)
    grad_padded, grad_vel_terms = pull_terms((lon_unpad(grad_in_padded), grad_tendency))
    grad_fields, grad_vel_stack = pull_stack(lon_unpad(grad_padded))
    local_grads = (
        grad_lift_w,
        grad_lift_b,
        jnp.stack(gains_list[::-1]),
        jnp.stack(shifts_list[::-1]),
        jnp.stack(kernels_list[::-1]),
        grad_qkv,
        grad_out,
        grad_head_w,
        grad_head_b,
    )
    return (grad_fields, grad_vel_terms + grad_vel_stack, local_grads)


def on_device(
    fields,
    velocity,
    context,
    masks,
    window,
    lift_weight,
    lift_bias,
    norm_gain,
    norm_shift,
    conv_weight,
    attn_qkv,
    attn_out,
    head_weight,
    head_bias,
    cot_fields,
    cot_velocity,
):
    params = (
        lift_weight,
        lift_bias,
        norm_gain,
        norm_shift,
        conv_weight,
        attn_qkv,
        attn_out,
        head_weight,
        head_bias,
    )
    weight_mask = masks.astype(jnp.float32)

    def evaluate(state_pair):
        return velocity_field(state_pair[0], state_pair[1], context, weight_mask, window, params)

    factors = (0.5, 0.5, 1.0)
    starts = [(fields, velocity)]
    slopes, records = ([], [])
    for section_index in range(4):
        slope_pair, record = evaluate(starts[-1])
        slopes.append(slope_pair)
        records.append(record)
        if section_index < 3:
            starts.append(
                (
                    fields + step_size * factors[section_index] * slope_pair[0],
                    velocity + step_size * factors[section_index] * slope_pair[1],
                )
            )
    new_fields = fields + step_size / 6.0 * (
        slopes[0][0] + 2.0 * slopes[1][0] + 2.0 * slopes[2][0] + slopes[3][0]
    )
    new_velocity = velocity + step_size / 6.0 * (
        slopes[0][1] + 2.0 * slopes[1][1] + 2.0 * slopes[2][1] + slopes[3][1]
    )
    grad_slopes = [
        (weight_rk * step_size / 6.0 * cot_fields, weight_rk * step_size / 6.0 * cot_velocity)
        for weight_rk in (1.0, 2.0, 2.0, 1.0)
    ]
    grad_fields, grad_velocity = (cot_fields, cot_velocity)
    totals = None
    for section_index in (3, 2, 1, 0):
        record = evaluate(starts[section_index])[1]
        back_fields, back_velocity, local_grads = velocity_back(
            record, weight_mask, grad_slopes[section_index][0], grad_slopes[section_index][1]
        )
        grad_fields = grad_fields + back_fields
        grad_velocity = grad_velocity + back_velocity
        if section_index > 0:
            factor_now = step_size * factors[section_index - 1]
            grad_slopes[section_index - 1] = (
                grad_slopes[section_index - 1][0] + factor_now * back_fields,
                grad_slopes[section_index - 1][1] + factor_now * back_velocity,
            )
        totals = (
            local_grads
            if totals is None
            else jax.tree.map(jnp.add, tuple(totals), tuple(local_grads))
        )
    totals = lax.psum(
        (
            totals[0],
            totals[1],
            totals[2],
            totals[3],
            totals[4],
            totals[5],
            totals[6],
            totals[7],
            totals[8],
        ),
        ("lon", "batch"),
    )
    return (
        new_fields,
        new_velocity,
        grad_fields,
        grad_velocity,
        totals[0],
        totals[1],
        totals[2],
        totals[3],
        totals[4],
        totals[5],
        totals[6],
        totals[7],
        totals[8],
    )


def solution(mesh):
    return jax.shard_map(
        on_device,
        mesh=mesh,
        in_specs=(
            P("batch", None, "lon", None),
            P("batch", None, "lon", None),
            P("batch", None, "lon", None),
            P("batch", None, "lon"),
            P(None, "lon", None),
            P(),
            P(),
            P(),
            P(),
            P(),
            P(),
            P(),
            P(),
            P(),
            P("batch", None, "lon", None),
            P("batch", None, "lon", None),
        ),
        out_specs=(
            P("batch", None, "lon", None),
            P("batch", None, "lon", None),
            P("batch", None, "lon", None),
            P("batch", None, "lon", None),
            P(),
            P(),
            P(),
            P(),
            P(),
            P(),
            P(),
            P(),
            P(),
        ),
        check_vma=False,
    )
```

profile of v0, /device:TPU:0, one launch (start us, length us, event | category | flops | bytes accessed | tf_op | source)
XLA Modules:
  0.0 2379.3 jit_solution(13955289288575493973)
XLA Ops:
  36.1 39.7 %all-reduce.80 = (f32[128]{0:T(128)S(1)}, f32[]{:T(128)}, f32[128]{0:T(128)S(1)}) all-reduce(f32[128]{0:T(128)S(1)} %get-tuple-element.577, f32[]{:T(128)} %convert_reduce_fusion, f32[128]{0:T(128)S(1)} %get-tuple-element.576), channel_id=1, replica_groups=mesh['lon'=4,'batch'=8] {'lon','batch'}, use_global_device_ids=true, to_apply=%region_1.2 | all-reduce | flops 257 | bytes 2056 | tf_op jit(solution)/shard_map/psum | solution.py:145
  91.0 40.3 %all-reduce.79 = (f32[128]{0:T(128)S(1)}, f32[128]{0:T(128)S(1)}) all-reduce(f32[128]{0:T(128)S(1)} %get-tuple-element.575, f32[128]{0:T(128)S(1)} %get-tuple-element.574), channel_id=1, replica_groups=mesh['lon'=4,'batch'=8] {'lon','batch'}, use_global_device_ids=true, to_apply=%region_7.8 | all-reduce | flops 256 | bytes 2048 | tf_op jit(solution)/shard_map/psum | solution.py:145
  284.1 38.5 %all-reduce.78 = (f32[128]{0:T(128)S(1)}, f32[128]{0:T(128)S(1)}) all-reduce(f32[128]{0:T(128)S(1)} %get-tuple-element.573, f32[128]{0:T(128)S(1)} %get-tuple-element.572), channel_id=1, replica_groups=mesh['lon'=4,'batch'=8] {'lon','batch'}, use_global_device_ids=true, to_apply=%region_13.15 | all-reduce | flops 256 | bytes 2048 | tf_op jit(solution)/shard_map/psum | solution.py:145
  338.0 40.4 %all-reduce.77 = (f32[128]{0:T(128)S(1)}, f32[128]{0:T(128)S(1)}) all-reduce(f32[128]{0:T(128)S(1)} %get-tuple-element.571, f32[128]{0:T(128)S(1)} %get-tuple-element.570), channel_id=1, replica_groups=mesh['lon'=4,'batch'=8] {'lon','batch'}, use_global_device_ids=true, to_apply=%region_17.19 | all-reduce | flops 256 | bytes 2048 | tf_op jit(solution)/shard_map/psum | solution.py:145
  483.1 17.6 fusion.22
  542.9 38.4 %all-reduce.76 = (f32[128]{0:T(128)S(1)}, f32[128]{0:T(128)S(1)}) all-reduce(f32[128]{0:T(128)S(1)} %get-tuple-element.569, f32[128]{0:T(128)S(1)} %get-tuple-element.568), channel_id=1, replica_groups=mesh['lon'=4,'batch'=8] {'lon','batch'}, use_global_device_ids=true, to_apply=%region_23.25 | all-reduce | flops 256 | bytes 2048 | tf_op jit(solution)/shard_map/psum | solution.py:145
  614.3 40.8 %all-reduce.75 = (f32[128]{0:T(128)S(1)}, f32[128]{0:T(128)S(1)}) all-reduce(f32[128]{0:T(128)S(1)} %get-tuple-element.567, f32[128]{0:T(128)S(1)} %get-tuple-element.566), channel_id=1, replica_groups=mesh['lon'=4,'batch'=8] {'lon','batch'}, use_global_device_ids=true, to_apply=%region_27.29 | all-reduce | flops 256 | bytes 2048 | tf_op jit(solution)/shard_map/psum | solution.py:145
  812.6 38.0 %all-reduce.74 = (f32[128]{0:T(128)S(1)}, f32[128]{0:T(128)S(1)}) all-reduce(f32[128]{0:T(128)S(1)} %get-tuple-element.565, f32[128]{0:T(128)S(1)} %get-tuple-element.564), channel_id=1, replica_groups=mesh['lon'=4,'batch'=8] {'lon','batch'}, use_global_device_ids=true, to_apply=%region_33.35 | all-reduce | flops 256 | bytes 2048 | tf_op jit(solution)/shard_map/psum | solution.py:145
  872.5 40.8 %all-reduce.73 = (f32[128]{0:T(128)S(1)}, f32[128]{0:T(128)S(1)}) all-reduce(f32[128]{0:T(128)S(1)} %get-tuple-element.563, f32[128]{0:T(128)S(1)} %get-tuple-element.562), channel_id=1, replica_groups=mesh['lon'=4,'batch'=8] {'lon','batch'}, use_global_device_ids=true, to_apply=%region_37.39 | all-reduce | flops 256 | bytes 2048 | tf_op jit(solution)/shard_map/psum | solution.py:145
  1051.5 18.2 fusion.6
  1108.5 23.9 %scatter_custom_fusion = f32[576,256]{1,0:T(8,128)} fusion(s32[4096]{0:T(1024)} %get-tuple-element.917, f32[4096,256]{1,0:T(8,128)} %reshape.3145, f32[]{:T(128)} %constant.956.clone.1), kind=kCustom, calls=%fused_computation.605 | custom fusion | flops 1048576 | bytes 590336 | tf_op jit(solution)/shard_map/transpose(jvp(jit(_take)))/scatter-add | solution.py:105
  1176.3 38.2 %all-reduce.72 = (f32[128]{0:T(128)S(1)}, f32[128]{0:T(128)S(1)}) all-reduce(f32[128]{0:T(128)S(1)} %fusion.590, f32[128]{0:T(128)S(1)} %get-tuple-element.714), channel_id=1, replica_groups=mesh['lon'=4,'batch'=8] {'lon','batch'}, use_global_device_ids=true, to_apply=%region_48.51 | all-reduce | flops 256 | bytes 2048 | tf_op jit(solution)/shard_map/psum | solution.py:197
  1230.0 41.4 %all-reduce.71 = (f32[128]{0:T(128)S(1)}, f32[128]{0:T(128)S(1)}) all-reduce(f32[128]{0:T(128)S(1)} %fusion.591, f32[128]{0:T(128)S(1)} %get-tuple-element.708), channel_id=1, replica_groups=mesh['lon'=4,'batch'=8] {'lon','batch'}, use_global_device_ids=true, to_apply=%region_52.55 | all-reduce | flops 256 | bytes 2048 | tf_op jit(solution)/shard_map/psum | solution.py:197
  1436.6 23.7 scatter_custom_fusion.1
  1488.4 38.6 %all-reduce.70 = (f32[128]{0:T(128)S(1)}, f32[128]{0:T(128)S(1)}) all-reduce(f32[128]{0:T(128)S(1)} %fusion.592, f32[128]{0:T(128)S(1)} %get-tuple-element.702), channel_id=1, replica_groups=mesh['lon'=4,'batch'=8] {'lon','batch'}, use_global_device_ids=true, to_apply=%region_60.63 | all-reduce | flops 256 | bytes 2048 | tf_op jit(solution)/shard_map/psum | solution.py:197
  1540.8 41.4 %all-reduce.69 = (f32[128]{0:T(128)S(1)}, f32[128]{0:T(128)S(1)}) all-reduce(f32[128]{0:T(128)S(1)} %fusion.593, f32[128]{0:T(128)S(1)} %get-tuple-element.696), channel_id=1, replica_groups=mesh['lon'=4,'batch'=8] {'lon','batch'}, use_global_device_ids=true, to_apply=%region_64.67 | all-reduce | flops 256 | bytes 2048 | tf_op jit(solution)/shard_map/psum | solution.py:197
  1742.8 23.7 scatter_custom_fusion.2
  1795.2 38.6 %all-reduce.68 = (f32[128]{0:T(128)S(1)}, f32[128]{0:T(128)S(1)}) all-reduce(f32[128]{0:T(128)S(1)} %fusion.594, f32[128]{0:T(128)S(1)} %get-tuple-element.688), channel_id=1, replica_groups=mesh['lon'=4,'batch'=8] {'lon','batch'}, use_global_device_ids=true, to_apply=%region_72.75 | all-reduce | flops 256 | bytes 2048 | tf_op jit(solution)/shard_map/psum | solution.py:197
  1848.4 41.3 %all-reduce.67 = (f32[128]{0:T(128)S(1)}, f32[128]{0:T(128)S(1)}) all-reduce(f32[128]{0:T(128)S(1)} %fusion.595, f32[128]{0:T(128)S(1)} %get-tuple-element.682), channel_id=1, replica_groups=mesh['lon'=4,'batch'=8] {'lon','batch'}, use_global_device_ids=true, to_apply=%region_76.79 | all-reduce | flops 256 | bytes 2048 | tf_op jit(solution)/shard_map/psum | solution.py:197
  2051.3 23.2 scatter_custom_fusion.3
  2106.3 38.5 %all-reduce.66 = (f32[128]{0:T(128)S(1)}, f32[128]{0:T(128)S(1)}) all-reduce(f32[128]{0:T(128)S(1)} %fusion.596, f32[128]{0:T(128)S(1)} %get-tuple-element.674), channel_id=1, replica_groups=mesh['lon'=4,'batch'=8] {'lon','batch'}, use_global_device_ids=true, to_apply=%region_84.87 | all-reduce | flops 256 | bytes 2048 | tf_op jit(solution)/shard_map/psum | solution.py:197
  2163.2 41.4 %all-reduce.65 = (f32[128]{0:T(128)S(1)}, f32[128]{0:T(128)S(1)}) all-reduce(f32[128]{0:T(128)S(1)} %fusion.597, f32[128]{0:T(128)S(1)} %get-tuple-element.668), channel_id=1, replica_groups=mesh['lon'=4,'batch'=8] {'lon','batch'}, use_global_device_ids=true, to_apply=%region_88.91 | all-reduce | flops 256 | bytes 2048 | tf_op jit(solution)/shard_map/psum | solution.py:197
  2265.7 38.6 %all-reduce.64 = (f32[128]{0:T(128)}, f32[2,128]{1,0:T(2,128)}, f32[2,128]{1,0:T(2,128)}, f32[128,10]{0,1:T(8,128)}, f32[10]{0:T(128)}) all-reduce(f32[128]{0:T(128)S(1)} %add_add_fusion.9, f32[2,128]{1,0:T(2,128)S(1)} %fusion.563, f32[2,128]{1,0:T(2,128)S(1)} %fusion.565, ...), channel_id=1, replica_groups=mesh['lon'=4,'batch'=8] {'lon','batch'}, use_global_device_ids=true, to_apply=%region_95.98 | all-reduce | flops 1930 | bytes 15440 | tf_op jit(solution)/shard_map/psum | solution.py:301
  2319.6 47.2 %all-reduce.84.cloned.1.call-done = (f32[3,3,100,128]{3,2,1,0:T(8,128)}, f32[2,3,3,128,128]{4,3,2,1,0:T(8,128)}, f32[128,384]{1,0:T(8,128)}, f32[128,128]{1,0:T(8,128)}) async-done(((f32[3,3,100,128]{3,2,1,0:T(8,128)}, f32[2,3,3,128,128]{4,3,2,1,0:T(8,128)}, f32[128,384]{1,0:T(8,128)}, f32[128,128]{1,0:T(8,128)}), (f32[3,3,100,128]{3,2,1,0:T(8,128)}, f32[2,3,3,128,128]{4,3,2,1,0:T(8,128)}, ...) | async-done | bytes 1902608 | tf_op jit(solution)/shard_map/psum | solution.py:301
  (1833 shorter events, 1505.2 us)
Async XLA Ops:
  7.2 2359.5 %all-reduce.84.cloned.1.call-start = ((), (), s32[]{:S(2)}) async-start(), calls=%async_computation | async-start | bytes 3842048 | tf_op jit(solution)/shard_map/psum | solution.py:301
  588.3 20.3 collective-permute-start.25
  589.6 19.0 collective-permute-start.24
  776.0 13.0 collective-permute-start.30
  777.6 11.3 collective-permute-start.31
  856.3 11.6 collective-permute-start.35
  857.4 10.6 collective-permute-start.34
  928.0 18.2 collective-permute-start.39
  928.9 17.3 collective-permute-start.38
  1134.5 21.5 collective-permute-start.40
  1282.1 13.3 collective-permute-start.46
  1293.7 17.7 collective-permute-start.47
  1326.1 10.6 collective-permute-start.48
  1592.2 13.3 collective-permute-start.56
  1603.8 17.6 collective-permute-start.57
  1899.7 13.4 collective-permute-start.66
  1911.3 17.4 collective-permute-start.67
  2091.3 11.9 collective-permute-start.72
  2093.4 9.9 collective-permute-start.73
  2149.7 10.4 collective-permute-start.74
  2149.8 10.5 collective-permute-start.75
  2214.1 20.1 collective-permute-start.76
  2216.1 34.0 %collective-permute-start.77 = (f32[1,32,1,100]{3,1,2,0:T(8,128)S(1)}, f32[1,32,1,100]{3,1,2,0:T(8,128)S(1)}, u32[]{:S(2)}, u32[]{:S(2)}) collective-permute-start(f32[1,32,1,100]{3,1,2,0:T(8,128)S(1)} %copy.1089), channel_id=1, source_target_pairs={{8,0},{16,8},{24,16},{0,24},{9,1},{17,9},{25,17},{1,25},{10,2},{18... | collective-permute-start | bytes 38408 | tf_op jit(solution)/shard_map/ppermute | solution.py:25
  2264.9 40.9 %collective-permute-start.78 = (f32[1,32,1,15]{2,3,1,0:T(8,128)}, f32[1,32,1,15]{2,3,1,0:T(8,128)}, u32[]{:S(2)}, u32[]{:S(2)}) collective-permute-start(f32[1,32,1,15]{2,3,1,0:T(8,128)} %get-tuple-element.843), channel_id=1, source_target_pairs={{0,8},{8,16},{16,24},{24,0},{1,9},{9,17},{17,25},{25,1},{2,10},{10... | collective-permute-start | bytes 5768 | tf_op jit(solution)/shard_map/ppermute | solution.py:22
  (479 other events, 5378.9 us)
Sparse Core Ops, SparseCore 0:
  2232.5 134.2 all-reduce.83
where the time goes:
time: 2400 us; the launch traced here: 2380 us
  blocking collectives  675 us (28%)
  local copies, waits for them, and re-layouts  655 us (27%)
  matrix products  475 us (20%)
  other arithmetic  383 us (16%)
  waiting for transfers between devices  104 us (4%)
  starting transfers between devices  65.4 us (3%)
    psum x8, blocking collectives, velocity_back(): lax.psum((grad_first, grad_second), ('lon', 'batch'))  319 us
    psum x8, blocking collectives, velocity_field(): lax.psum((jnp.sum(weighted, axis=(0, 1, 2)), jnp.sum(weighted * hidden, a...  317 us
    conv_general_dilated x36, matrix products, conv_same(): lax.conv_general_dilated(padded, kernel, (1, 1), ((1, 1), (0, 0)), dimens...  167 us
    dot_general x8, matrix products, attend(): jnp.einsum('abchw,abcwhd->abchd', weights, picked[..., 1, :, :], precisio...  138 us
    dot_general x8, matrix products, attend(): jnp.einsum('abchd,abcwhd->abchw', heads_query, picked[..., 0, :, :], prec...  125 us
    reshape x8, local copies, waits for them, and re-layouts, attend(): picked.reshape(samples, lat_count, lon_count, keys_count, 2, HEADS, head_...  113 us
    scatter-add x4, other arithmetic, attend(): picked = jnp.take(flat_pairs, flat_index.reshape(-1), axis=1)  94.5 us
    another operation x32, local copies, waits for them, and re-layouts  92.2 us
  transfers between devices with their start and end apart: 81, of which 36 were waited for; matrix products, arithmetic and copies ran while one was open for 14% of the time, Pallas kernels for 0%

commit v1 on v0

v1 whole, which is shorter than its diff:
```python
from functools import partial
import math

import jax
import jax.numpy as jnp
from jax import lax
from jax.experimental import pallas as pl
from jax.experimental.pallas import tpu as pltpu
from jax.sharding import PartitionSpec as P

HEADS = 4
SECTIONS = 4
LANES = 128
VARS = 5
MASK_LANE = 127
epsilon = 1e-05
step_size = 0.25
f32 = jnp.float32
bf16 = jnp.bfloat16
MESH = pl.DeviceIdType.MESH


def split(x):
    hi = x.astype(bf16)
    return hi, (x - hi.astype(f32)).astype(bf16)


def dot(a, b, dims=((1,), (0,))):
    return lax.dot_general(a, b, (dims, ((), ())), preferred_element_type=f32)


def lanes_cat(*parts):
    return jnp.concatenate(parts, axis=1)


def factors(n):
    out = []
    while n > 4 and n % 2 == 0:
        out.append(2)
        n //= 2
    if n > 1:
        out.append(n)
    return out


def kernel(
    sizes,
    start_ref,
    window_ref,
    small_ref,
    lift_ref,
    conv_ref,
    qkv_ref,
    out_ref,
    head_ref,
    new_ref,
    grad_ref,
    weights_out,
    norm_out,
    ys,
    xh,
    xl,
    h0,
    h1,
    a1h,
    a1l,
    a2h,
    a2l,
    dg1,
    dg2,
    h2h,
    h2l,
    qh,
    ql,
    kh,
    kl,
    vh,
    vl,
    probs,
    bh,
    bl,
    h3h,
    h3l,
    norms,
    gk,
    acc,
    tend,
    mask,
    mult,
    w3f,
    w3t,
    wq3,
    wqt3,
    wo3,
    wot3,
    wh3,
    wht3,
    tap,
    blend,
    dbh,
    dbl,
    dq,
    dkv,
    dh2,
    de1,
    de0,
    sb,
    rb,
    gw,
    rsb,
    norm_acc,
    bias_acc,
    ar_src,
    ar_buf,
    ar_send,
    ar_recv,
    halo_send,
    halo_recv,
    rs_send,
    rs_recv,
    ag_send,
    ag_recv,
):
    nl, nb, L, W, hid_heads = sizes
    nd = nl * nb
    R = L * W
    R1 = R + 2 * L
    R2 = R + 4 * L
    ch = LANES
    me_l = lax.axis_index("lon")
    me_b = lax.axis_index("batch")
    me = me_l * nb + me_b
    left = (lax.rem(me_l + nl - 1, nl), me_b)
    right = (lax.rem(me_l + 1, nl), me_b)

    def peer(k):
        t = lax.rem(me + k, nd)
        return (t // nb, lax.rem(t, nb))

    barrier = pltpu.get_barrier_semaphore()

    def greet(k, c):
        pl.semaphore_signal(barrier, inc=1, device_id=peer(k), device_id_type=MESH)
        return c

    lax.fori_loop(1, nd, greet, 0)

    def sum_start(a, vals):
        ar_src[a] = vals
        ar_buf[a, me] = vals

        def send(k, c):
            pltpu.make_async_remote_copy(
                ar_src.at[a],
                ar_buf.at[a, me],
                ar_send.at[a],
                ar_recv.at[a],
                device_id=peer(k),
                device_id_type=MESH,
            ).start()
            return c

        lax.fori_loop(1, nd, send, 0)

    def sum_wait(a):
        got = ar_buf.at[a, pl.ds(0, nd - 1)]
        pltpu.make_async_copy(got, got, ar_recv.at[a]).wait()
        pltpu.make_async_copy(got, got, ar_send.at[a]).wait()
        return jnp.sum(ar_buf[a], axis=0)

    def side_copy(h, side, src, dst):
        return pltpu.make_async_remote_copy(
            src,
            dst,
            halo_send.at[h, side],
            halo_recv.at[h, side],
            device_id=left if side == 0 else right,
            device_id_type=MESH,
        )

    def halo_copies(h, buf, s, cols):
        n = cols * L
        lo = 2 * L - n
        to_left = side_copy(
            h, 0, buf.at[s, pl.ds(2 * L, n)], buf.at[s, pl.ds(R + 2 * L, n)]
        )
        to_right = side_copy(
            h, 1, buf.at[s, pl.ds(R + 2 * L - n, n)], buf.at[s, pl.ds(lo, n)]
        )
        return to_left, to_right

    def halo_start(h, buf, s, cols):
        for c in halo_copies(h, buf, s, cols):
            c.start()

    def halo_wait(h, buf, s, cols):
        for c in halo_copies(h, buf, s, cols):
            c.wait()

    def lat_of(n):
        return lax.broadcasted_iota(jnp.int32, (n, LANES), 0) % L

    def north(x):
        n = x.shape[0]
        return jnp.where(lat_of(n) == L - 1, 0.0, pltpu.roll(x, n - 1, 0))

    def south(x):
        n = x.shape[0]
        return jnp.where(lat_of(n) == 0, 0.0, pltpu.roll(x, 1, 0))

    def lat_diff(x):
        return 0.5 * (north(x) - south(x))

    def lane_of(n):
        return lax.broadcasted_iota(jnp.int32, (n, LANES), 1)

    def lroll(x, shift):
        return pltpu.roll(x, shift % LANES, 1)

    def conv(hi, lo, base, n, weights):
        cols_h = [hi[base + j * L : base + j * L + n] for j in range(3)]
        cols_l = [lo[base + j * L : base + j * L + n] for j in range(3)]
        wide = dot(lanes_cat(*cols_h, *cols_l, *cols_h), weights)
        return (
            wide[:, ch : 2 * ch]
            + south(wide[:, :ch])
            + north(wide[:, 2 * ch :])
        )

    def product(x, weights):
        hi, lo = split(x)
        return dot(lanes_cat(hi, lo, hi), weights)

    def rows_product(ah, al, gh, gl):
        t = ((0,), (0,))
        return dot(ah, gh, t) + dot(ah, gl, t) + dot(al, gh, t)

    def lat_triple(x):
        return split(lanes_cat(north(x), x, south(x)))

    def conv_back(gh, gl, n, weights):
        wide = dot(lanes_cat(gh, gl, gh), weights)
        return (
            wide[2 * L : 2 * L + n, :ch]
            + wide[L : L + n, ch : 2 * ch]
            + wide[:n, 2 * ch :]
        )

    def add_conv_grad(base, ah, al, gh, gl):
        for j in range(3):
            part = rows_product(
                ah[j * L : j * L + R], al[j * L : j * L + R], gh, gl
            )
            for i in range(3):
                at = base + (i * 3 + j) * ch
                gw[at : at + ch, :] += part[:, i * ch : (i + 1) * ch]

    lift_base, conv_base = 0, 9 * ch
    qkv_base = 27 * ch
    out_base, head_base = 30 * ch, 31 * ch

    ys[0, 2 * L : 2 * L + R] = start_ref[:, :ch]
    cot = start_ref[:, ch:]
    for s, weight in enumerate((1.0, 2.0, 2.0, 1.0)):
        gk[s] = cot * (weight * step_size / 6.0)
    grad_ref[...] = cot
    acc[...] = jnp.zeros_like(acc)
    gw[...] = jnp.zeros_like(gw)
    norm_acc[...] = jnp.zeros_like(norm_acc)
    bias_acc[...] = jnp.zeros_like(bias_acc)
    mask_own = jnp.broadcast_to(
        start_ref[:, MASK_LANE : MASK_LANE + 1], (R, LANES)
    )
    count_part = jnp.sum(mask_own, axis=0, keepdims=True)

    pl.semaphore_wait(barrier, nd - 1)
    halo_start(0, ys, 0, 2)
    sum_start(4 * SECTIONS, jnp.concatenate([count_part, count_part], axis=0))

    tap[...] = jnp.zeros_like(tap)
    for b in range(3):
        for i in range(3):
            for j in range(3):
                if b == 0:
                    tap[: lift_ref.shape[2]] = lift_ref[i, j]
                    w = tap[...]
                else:
                    w = conv_ref[b - 1, i, j]
                hi, lo = split(w)
                for p, part in enumerate((hi, hi, lo)):
                    at = (p * 3 + j) * ch
                    w3f[b, at : at + ch, i * ch : (i + 1) * ch] = part
                hi, lo = split(w.T)
                for p, part in enumerate((hi, hi, lo)):
                    at = (p * 3 + i) * ch
                    w3t[b, at : at + ch, j * ch : (j + 1) * ch] = part

    def put_three(target, w):
        n = w.shape[0]
        hi, lo = split(w)
        target[:n] = hi
        target[n : 2 * n] = hi
        target[2 * n :] = lo

    put_three(wq3, qkv_ref[...])
    put_three(wqt3, qkv_ref[...].T)
    put_three(wo3, out_ref[...])
    put_three(wot3, out_ref[...].T)
    put_three(wh3, head_ref[...])
    put_three(wht3, head_ref[...].T)

    counted = jnp.zeros((R, LANES), f32)
    key_of = lane_of(R)
    for k in range(window_ref.shape[1]):
        entry = jnp.broadcast_to(window_ref[:, k : k + 1], (R, LANES))
        counted = counted + jnp.where(entry == key_of, 1.0, 0.0)
    mult[...] = counted.reshape(W, L, LANES)
    for s in range(SECTIONS):
        for ref in (kh, kl, vh, vl):
            ref[s, R1:] = jnp.zeros((L, ch), bf16)

    head_rows = lax.broadcasted_iota(jnp.int32, (HEADS * L, ch), 0) // L
    head_lanes = lax.broadcasted_iota(jnp.int32, (HEADS * L, ch), 1) // (ch // HEADS)
    head_mask = jnp.where(head_rows == head_lanes, 1.0, 0.0)
    head_mask_h = head_mask.astype(bf16)
    scale = (ch // HEADS) ** -0.5

    def per_head(x):
        return jnp.concatenate([x] * HEADS, axis=0) * head_mask_h

    def heads_sum(x):
        x = x * head_mask
        return sum(x[h * L : (h + 1) * L] for h in range(1, HEADS)) + x[:L]

    total_count = sum_wait(4 * SECTIONS)[0:1]
    inverse_count = 1.0 / total_count

    lift_bias = small_ref[0:1]
    head_bias = small_ref[1:2]
    gains = [small_ref[2:3], small_ref[3:4]]
    shifts = [small_ref[4:5], small_ref[5:6]]

    def stats(h):
        weighted = h * mask[2 * L : 2 * L + R]
        return jnp.concatenate(
            [
                jnp.sum(weighted, axis=0, keepdims=True),
                jnp.sum(weighted * h, axis=0, keepdims=True),
            ],
            axis=0,
        )

    def normalise(s, b, sums):
        average = sums[0:1] / total_count
        spread = sums[1:2] / total_count - average * average
        inverse = lax.rsqrt(spread + epsilon)
        norms[s, b, 0:1] = average
        norms[s, b, 1:2] = inverse
        return average, inverse

    def activity(h, b, average, inverse):
        z = (h - average) * inverse * gains[b] + shifts[b]
        below = 0.5 * (1.0 + lax.erf(z * (0.5**0.5)))
        slope = below + z * (
            jnp.exp(-0.5 * z * z) * (1.0 / math.sqrt(2.0 * math.pi))
        )
        return z * below, slope

    group = 4

    def forward(s, carry):
        hb = s * 6

        @pl.when(s > 0)
        def _():
            halo_start(hb, ys, s, 2)

        halo_wait(hb, ys, s, 2)

        @pl.when(s == 0)
        def _():
            mask[...] = jnp.broadcast_to(
                ys[0, :, MASK_LANE : MASK_LANE + 1], (R2, LANES)
            )

        y1 = ys[s, L : L + R1]
        lane = lane_of(R1)
        lon = 0.5 * (ys[s, 2 * L : 2 * L + R1] - ys[s, 0:R1])
        x = jnp.where(
            (lane >= VARS) & (lane < 2 * VARS),
            lat_diff(y1),
            jnp.where((lane >= 2 * VARS) & (lane < 3 * VARS), lon, y1),
        )
        hi, lo = split(x)
        xh[s] = hi
        xl[s] = lo
        flux = y1 * lroll(y1, -3 * VARS)
        flux = jnp.where(lane < 2 * VARS, flux, 0.0)
        own_lane = lane_of(R)
        t_lat = jnp.where(own_lane < VARS, lat_diff(flux[L : L + R]), 0.0)
        t_lon = jnp.where(
            own_lane >= VARS, 0.5 * (flux[2 * L : 2 * L + R] - flux[:R]), 0.0
        )
        t = -(t_lat + lroll(t_lon, -VARS))
        tend[...] = t + lroll(t, VARS) + lroll(t, 2 * VARS)

        first = conv(xh.at[s], xl.at[s], 0, R, w3f[0]) + lift_bias
        h0[s, 2 * L : 2 * L + R] = first
        sum_start(s * 4, stats(first))
        halo_start(hb + 1, h0, s, 2)
        average, inverse = normalise(s, 0, sum_wait(s * 4))
        halo_wait(hb + 1, h0, s, 2)
        act, slope = activity(h0[s, L : L + R1], 0, average, inverse)
        dg1[s] = slope[L : L + R]
        hi, lo = split(act)
        a1h[s] = hi
        a1l[s] = lo
        second = h0[s, 2 * L : 2 * L + R] + conv(a1h.at[s], a1l.at[s], 0, R, w3f[1])
        h1[s, 2 * L : 2 * L + R] = second
        sum_start(s * 4 + 1, stats(second))
        halo_start(hb + 2, h1, s, 2)
        average, inverse = normalise(s, 1, sum_wait(s * 4 + 1))
        halo_wait(hb + 2, h1, s, 2)
        act, slope = activity(h1[s], 1, average, inverse)
        dg2[s] = slope[2 * L : 2 * L + R]
        hi, lo = split(act)
        a2h[s] = hi
        a2l[s] = lo
        third = h1[s, L : L + R1] + conv(a2h.at[s], a2l.at[s], 0, R1, w3f[2])
        hi, lo = split(third)
        h2h[s] = hi
        h2l[s] = lo
        mixing = dot(lanes_cat(hi, lo, hi), wq3[...])
        hi, lo = split(mixing[L : L + R, :ch] * scale)
        qh[s] = hi
        ql[s] = lo
        hi, lo = split(mixing[:, ch : 2 * ch])
        kh[s, :R1] = hi
        kl[s, :R1] = lo
        hi, lo = split(mixing[:, 2 * ch :])
        vh[s, :R1] = hi
        vl[s, :R1] = lo

        def attend(g, c):
            cols = [g * group + k for k in range(group)]
            scores = []
            for col in cols:
                at = pl.multiple_of(col * L, L)
                q_h = per_head(qh[s, pl.ds(at, L)])
                q_l = per_head(ql[s, pl.ds(at, L)])
                k_h = kh[s, pl.ds(at, 4 * L)]
                k_l = kl[s, pl.ds(at, 4 * L)]
                scores.append(
                    dot(
                        lanes_cat(q_h, q_l, q_h),
                        lanes_cat(k_h, k_h, k_l),
                        ((1,), (1,)),
                    )
                )
            weights = []
            for col, score in zip(cols, scores):
                m = jnp.concatenate([mult[col]] * HEADS, axis=0)
                score = jnp.where(m > 0.0, score, -1e30)
                top = jnp.max(score, axis=1, keepdims=True)
                e = m * jnp.exp(score - top)
                p = e / jnp.sum(e, axis=1, keepdims=True)
                probs[s, col] = p
                weights.append(p)
            for col, p in zip(cols, weights):
                at = pl.multiple_of(col * L, L)
                p_h, p_l = split(p)
                v_h = vh[s, pl.ds(at, 4 * L)]
                v_l = vl[s, pl.ds(at, 4 * L)]
                o = dot(
                    lanes_cat(p_h, p_l, p_h),
                    jnp.concatenate([v_h, v_h, v_l], axis=0),
                )
                blend[pl.ds(at, L)] = heads_sum(o)
            return c

        lax.fori_loop(0, W // group, attend, 0)
        hi, lo = split(blend[...])
        bh[s] = hi
        bl[s] = lo
        fourth = third[L : L + R] + dot(lanes_cat(hi, lo, hi), wo3[...])
        hi, lo = split(fourth)
        h3h[s] = hi
        h3l[s] = lo
        slope_now = (
            tend[...] + dot(lanes_cat(hi, lo, hi), wh3[...]) + head_bias
        )
        weight = jnp.where((s == 0) | (s == SECTIONS - 1), 1.0, 2.0)
        acc[...] += weight * slope_now

        @pl.when(s < SECTIONS - 1)
        def _():
            factor = jnp.where(s == SECTIONS - 2, 1.0, 0.5) * step_size
            ys[s + 1, 2 * L : 2 * L + R] = (
                ys[0, 2 * L : 2 * L + R] + factor * slope_now
            )

        return carry

    lax.fori_loop(0, SECTIONS, forward, 0)
    new_ref[...] = ys[0, 2 * L : 2 * L + R] + (step_size / 6.0) * acc[...]

    def norm_back(s, b, h, grad_act, slope, through):
        average = norms[s, b, 0:1]
        inverse = norms[s, b, 1:2]
        dz = grad_act * slope
        hat = (h - average) * inverse
        sums = jnp.concatenate(
            [
                jnp.sum(dz, axis=0, keepdims=True),
                jnp.sum(dz * hat, axis=0, keepdims=True),
            ],
            axis=0,
        )
        return sums, through + dz * (gains[b] * inverse)

    def norm_rest(s, b, h, weight_mask, direct, sums):
        average = norms[s, b, 0:1]
        inverse = norms[s, b, 1:2]
        hat = (h - average) * inverse
        norm_acc[b] += sums
        return direct - weight_mask * (
            gains[b] * inverse * inverse_count
        ) * (sums[0:1] + hat * sums[1:2])

    def backward(turn, carry):
        s = SECTIONS - 1 - turn
        hb = s * 6
        g = gk[s]
        g_h, g_l = split(g)
        grad3 = dot(lanes_cat(g_h, g_l, g_h), wht3[...])
        bias_acc[1:2] += jnp.sum(g, axis=0, keepdims=True)
        gw[head_base : head_base + ch] += rows_product(h3h[s], h3l[s], g_h, g_l)
        hi, lo = split(grad3)
        gw[out_base : out_base + ch] += rows_product(bh[s], bl[s], hi, lo)
        hi, lo = split(dot(lanes_cat(hi, lo, hi), wot3[...]))
        dbh[...] = hi
        dbl[...] = lo
        dkv[...] = jnp.zeros_like(dkv)

        def attend_back(gi, c):
            cols = [gi * group + k for k in range(group)]
            dps = []
            for col in cols:
                at = pl.multiple_of(col * L, L)
                d_h = per_head(dbh[pl.ds(at, L)])
                d_l = per_head(dbl[pl.ds(at, L)])
                v_h = vh[s, pl.ds(at, 4 * L)]
                v_l = vl[s, pl.ds(at, 4 * L)]
                dps.append(
                    dot(
                        lanes_cat(d_h, d_l, d_h),
                        lanes_cat(v_h, v_h, v_l),
                        ((1,), (1,)),
                    )
                )
            dss = []
            for col, dp in zip(cols, dps):
                p = probs[s, col]
                mean = jnp.sum(p * dp, axis=1, keepdims=True)
                dss.append(p * (dp - mean))
            for col, ds in zip(cols, dss):
                at = pl.multiple_of(col * L, L)
                ds_h, ds_l = split(ds)
                k_h = kh[s, pl.ds(at, 4 * L)]
                k_l = kl[s, pl.ds(at, 4 * L)]
                o = dot(
                    lanes_cat(ds_h, ds_l, ds_h),
                    jnp.concatenate([k_h, k_h, k_l], axis=0),
                )
                dq[pl.ds(at, L)] = heads_sum(o) * scale
                q_h = per_head(qh[s, pl.ds(at, L)])
                q_l = per_head(ql[s, pl.ds(at, L)])
                t_h, t_l = split(ds.T)
                dkv[pl.ds(at, 4 * L), :ch] += dot(
                    lanes_cat(t_h, t_l, t_h),
                    jnp.concatenate([q_h, q_h, q_l], axis=0),
                )
                t_h, t_l = split(probs[s, col].T)
                d_h = per_head(dbh[pl.ds(at, L)])
                d_l = per_head(dbl[pl.ds(at, L)])
                dkv[pl.ds(at, 4 * L), ch:] += dot(
                    lanes_cat(t_h, t_l, t_h),
                    jnp.concatenate([d_h, d_h, d_l], axis=0),
                )
            return c

        lax.fori_loop(0, W // group, attend_back, 0)
        zeros = jnp.zeros((L, ch), f32)
        d_all = lanes_cat(
            jnp.concatenate([zeros, dq[...], zeros], axis=0), dkv[:R1]
        )
        d_h, d_l = split(d_all)
        part = dot(lanes_cat(d_h, d_l, d_h), wqt3[...])
        dh2[...] = part + jnp.concatenate([zeros, grad3, zeros], axis=0)
        sb[s, 0, : 2 * L] = dh2[: 2 * L]
        sb[s, 0, 2 * L :] = gk[s, :L]
        sb[s, 1, : 2 * L] = dh2[R:]
        sb[s, 1, 2 * L :] = gk[s, R - L :]
        edges = [
            side_copy(hb + 3, side, sb.at[s, side], rb.at[s, side])
            for side in range(2)
        ]
        for e in edges:
            e.start()
        wide = rows_product(h2h[s], h2l[s], d_h, d_l)
        for k in range(3):
            at = qkv_base + k * ch
            gw[at : at + ch] += wide[:, k * ch : (k + 1) * ch]
        for e in edges:
            e.wait()
        dh2[: 2 * L] += rb[s, 1, : 2 * L]
        dh2[R:] += rb[s, 0, : 2 * L]

        t_h, t_l = lat_triple(dh2[...])
        grad_act = conv_back(t_h, t_l, R, w3t[2])
        sums, direct = norm_back(
            s, 1, h1[s, 2 * L : 2 * L + R], grad_act, dg2[s], dh2[L : L + R]
        )
        sum_start(s * 4 + 2, sums)
        de1[s, 2 * L : 2 * L + R] = direct
        halo_start(hb + 4, de1, s, 1)
        add_conv_grad(
            conv_base + 9 * ch,
            a2h[s, L : L + R1],
            a2l[s, L : L + R1],
            t_h[L : L + R],
            t_l[L : L + R],
        )
        sums = sum_wait(s * 4 + 2)
        halo_wait(hb + 4, de1, s, 1)
        grad1 = norm_rest(
            s, 1, h1[s, L : L + R1], mask[L : L + R1], de1[s, L : L + R1], sums
        )
        t_h, t_l = lat_triple(grad1)
        grad_act = conv_back(t_h, t_l, R, w3t[1])
        sums, direct = norm_back(
            s, 0, h0[s, 2 * L : 2 * L + R], grad_act, dg1[s], grad1[L : L + R]
        )
        sum_start(s * 4 + 3, sums)
        de0[s, 2 * L : 2 * L + R] = direct
        halo_start(hb + 5, de0, s, 2)
        add_conv_grad(
            conv_base, a1h[s], a1l[s], t_h[L : L + R], t_l[L : L + R]
        )
        sums = sum_wait(s * 4 + 3)
        halo_wait(hb + 5, de0, s, 2)
        grad0 = norm_rest(s, 0, h0[s], mask[...], de0[s], sums)
        bias_acc[0:1] += jnp.sum(grad0[2 * L : 2 * L + R], axis=0, keepdims=True)
        t_h, t_l = lat_triple(grad0)
        add_conv_grad(
            lift_base, xh[s], xl[s], t_h[2 * L : 2 * L + R], t_l[2 * L : 2 * L + R]
        )
        dx = conv_back(t_h, t_l, R1, w3t[0])
        lane = lane_of(R)
        own = dx[L : L + R]
        lon = 0.5 * (dx[2 * L :] - dx[:R])
        g = gk[s]
        g_lon = jnp.concatenate([g[L:], rb[s, 0, 2 * L :]], axis=0)
        g_lon = 0.5 * (
            g_lon - jnp.concatenate([rb[s, 1, 2 * L :], g[: R - L]], axis=0)
        )
        dflux = jnp.where(
            lane < VARS, lat_diff(g), jnp.where(lane < 2 * VARS, g_lon, 0.0)
        )
        y = ys[s, 2 * L : 2 * L + R]
        parts = jnp.where(
            lane < VARS,
            own,
            jnp.where(lane < 2 * VARS, -lat_diff(own), -lon),
        )
        parts = parts + dflux * lroll(y, -3 * VARS)
        parts = jnp.where(lane < 3 * VARS, parts, 0.0)
        fields_grad = (
            parts
            + lroll(parts, VARS)
            + lroll(parts, 2 * VARS)
            + lroll(parts, -VARS)
            + lroll(parts, -2 * VARS)
        )
        velocity_grad = own + lroll(dflux * y, 3 * VARS)
        gy = jnp.where(
            lane < 3 * VARS,
            fields_grad,
            jnp.where(lane < 5 * VARS, velocity_grad, 0.0),
        )
        grad_ref[...] += gy

        @pl.when(s > 0)
        def _():
            factor = jnp.where(s == SECTIONS - 1, 1.0, 0.5) * step_size
            gk[s - 1] = gk[s - 1] + factor * gy

        return carry

    lax.fori_loop(0, SECTIONS, backward, 0)

    gw[ch - 28 : ch - 27] = bias_acc[0:1]
    gw[ch - 27 : ch - 26] = bias_acc[1:2]
    norm_out[...] = norm_acc[...]

    stages = []
    step = 1
    for n in factors(nl):
        idx = lax.rem(me_l // step, n)

        def at(k, idx=idx, n=n, step=step):
            q = lax.rem(idx + k, n)
            return q, (me_l + (q - idx) * step, me_b)

        stages.append((n, idx, at))
        step *= n
    step = 1
    for n in factors(nb):
        idx = lax.rem(me_b // step, n)

        def at(k, idx=idx, n=n, step=step):
            q = lax.rem(idx + k, n)
            return q, (me_l, me_b + (q - idx) * step)

        stages.append((n, idx, at))
        step *= n
    size = gw.shape[0]
    off = 0
    slot = 0
    regions = []
    for t, (n, idx, at) in enumerate(stages):
        part = size // n
        for k in range(1, n):
            q, device = at(k)
            pltpu.make_async_remote_copy(
                gw.at[pl.ds(pl.multiple_of(off + q * part, 8), part)],
                rsb.at[pl.ds(slot + (n - 1 - k) * part, part)],
                rs_send.at[t],
                rs_recv.at[t],
                device_id=device,
                device_id_type=MESH,
            ).start()
        got = rsb.at[pl.ds(slot, (n - 1) * part)]
        pltpu.make_async_copy(got, got, rs_recv.at[t]).wait()
        pltpu.make_async_copy(got, got, rs_send.at[t]).wait()
        regions.append((off, size, part))
        off = off + idx * part
        chunk = math.gcd(part, 256)

        def add(i, c, off=off, slot=slot, n=n, part=part, chunk=chunk):
            at_row = pl.multiple_of(i * chunk, 8)
            total = gw[pl.ds(pl.multiple_of(off + at_row, 8), chunk)]
            for k in range(n - 1):
                total = total + rsb[
                    pl.ds(pl.multiple_of(slot + k * part + at_row, 8), chunk)
                ]
            gw[pl.ds(pl.multiple_of(off + at_row, 8), chunk)] = total
            return c

        lax.fori_loop(0, part // chunk, add, 0)
        slot += (n - 1) * part
        size = part
    weights_out[pl.ds(pl.multiple_of(off, 8), size)] = gw[
        pl.ds(pl.multiple_of(off, 8), size)
    ]
    for t in reversed(range(len(stages))):
        n, idx, at = stages[t]
        base, _, part = regions[t]
        mine = weights_out.at[pl.ds(pl.multiple_of(base + idx * part, 8), part)]
        for k in range(1, n):
            pltpu.make_async_remote_copy(
                mine,
                mine,
                ag_send.at[t],
                ag_recv.at[t],
                device_id=at(k)[1],
                device_id_type=MESH,
            ).start()
        got = rsb.at[pl.ds(0, (n - 1) * part)]
        pltpu.make_async_copy(got, got, ag_recv.at[t]).wait()
        pltpu.make_async_copy(got, got, ag_send.at[t]).wait()


def on_device(
    nl,
    nb,
    fields,
    velocity,
    context,
    masks,
    window,
    lift_weight,
    lift_bias,
    norm_gain,
    norm_shift,
    conv_weight,
    attn_qkv,
    attn_out,
    head_weight,
    head_bias,
    cot_fields,
    cot_velocity,
):
    _, L, W, _ = fields.shape
    R, R1, R2 = L * W, L * (W + 2), L * (W + 4)
    ch = LANES
    nd = nl * nb
    grid = (L, W)
    used = 3 * VARS + 2 * VARS + context.shape[-1]
    start = jnp.concatenate(
        [
            fields[0],
            fields[0],
            fields[0],
            velocity[0],
            context[0],
            jnp.zeros((*grid, MASK_LANE - used), f32),
            masks[0].astype(f32)[..., None],
            cot_fields[0],
            cot_fields[0],
            cot_fields[0],
            cot_velocity[0],
            jnp.zeros((*grid, ch - 5 * VARS), f32),
        ],
        axis=-1,
    )
    start = start.transpose(1, 0, 2).reshape(R, 2 * ch)
    keys = window.transpose(1, 0, 2).reshape(R, window.shape[-1])
    side = ((0, 0), (3 * VARS, ch - 5 * VARS))
    small = jnp.concatenate(
        [
            lift_bias[None],
            jnp.pad(head_bias[None], side),
            norm_gain,
            norm_shift,
            jnp.zeros((2, ch), f32),
        ],
        axis=0,
    )
    head = jnp.pad(head_weight, side)
    S = SECTIONS
    rows = 32 * ch
    rows = -(-rows // (8 * nd)) * 8 * nd
    stage_count = len(factors(nl)) + len(factors(nb))
    vm = pltpu.VMEM
    dma = pltpu.SemaphoreType.DMA
    scratch = [
        vm((S, R2, ch), f32),
        vm((S, R1, ch), bf16),
        vm((S, R1, ch), bf16),
        vm((S, R2, ch), f32),
        vm((S, R2, ch), f32),
        vm((S, R1, ch), bf16),
        vm((S, R1, ch), bf16),
        vm((S, R2, ch), bf16),
        vm((S, R2, ch), bf16),
        vm((S, R, ch), f32),
        vm((S, R, ch), f32),
        vm((S, R1, ch), bf16),
        vm((S, R1, ch), bf16),
        vm((S, R, ch), bf16),
        vm((S, R, ch), bf16),
        vm((S, R1 + L, ch), bf16),
        vm((S, R1 + L, ch), bf16),
        vm((S, R1 + L, ch), bf16),
        vm((S, R1 + L, ch), bf16),
        vm((S, W, HEADS * L, ch), f32),
        vm((S, R, ch), bf16),
        vm((S, R, ch), bf16),
        vm((S, R, ch), bf16),
        vm((S, R, ch), bf16),
        vm((S, 2, 8, ch), f32),
        vm((S, R, ch), f32),
        vm((R, ch), f32),
        vm((R, ch), f32),
        vm((R2, ch), f32),
        vm((W, L, ch), f32),
        vm((3, 9 * ch, 3 * ch), bf16),
        vm((3, 9 * ch, 3 * ch), bf16),
        vm((3 * ch, 3 * ch), bf16),
        vm((9 * ch, ch), bf16),
        vm((3 * ch, ch), bf16),
        vm((3 * ch, ch), bf16),
        vm((3 * ch, ch), bf16),
        vm((3 * ch, ch), bf16),
        vm((ch, ch), f32),
        vm((R, ch), f32),
        vm((R, ch), bf16),
        vm((R, ch), bf16),
        vm((R, ch), f32),
        vm((R1 + L, 2 * ch), f32),
        vm((R1, ch), f32),
        vm((S, R2, ch), f32),
        vm((S, R2, ch), f32),
        vm((S, 2, 3 * L, ch), f32),
        vm((S, 2, 3 * L, ch), f32),
        vm((rows, ch), f32),
        vm((rows, ch), f32),
        vm((2, 2, ch), f32),
        vm((2, ch), f32),
        vm((4 * S + 1, 2, ch), f32),
        vm((4 * S + 1, nd, 2, ch), f32),
        dma((4 * S + 1,)),
        dma((4 * S + 1,)),
        dma((6 * S, 2)),
        dma((6 * S, 2)),
        dma((stage_count,)),
        dma((stage_count,)),
        dma((stage_count,)),
        dma((stage_count,)),
    ]
    whole = pl.BlockSpec(memory_space=pltpu.VMEM)
    new, grad, weights, norm_grads = pl.pallas_call(
        partial(kernel, (nl, nb, L, W, HEADS)),
        out_shape=(
            jax.ShapeDtypeStruct((R, ch), f32),
            jax.ShapeDtypeStruct((R, ch), f32),
            jax.ShapeDtypeStruct((rows, ch), f32),
            jax.ShapeDtypeStruct((2, 2, ch), f32),
        ),
        in_specs=[whole] * 8,
        out_specs=(whole,) * 4,
        scratch_shapes=scratch,
        compiler_params=pltpu.CompilerParams(
            collective_id=0, has_side_effects=True, vmem_limit_bytes=60 * 2**20
        ),
    )(start, keys, small, lift_weight, conv_weight, attn_qkv, attn_out, head)

    def state(x):
        x = x.reshape(W, L, ch).transpose(1, 0, 2)[None]
        return x[..., :VARS], x[..., 3 * VARS : 5 * VARS]

    new_fields, new_velocity = state(new)
    grad_fields, grad_velocity = state(grad)
    cin = lift_weight.shape[2]
    vel = slice(3 * VARS, 5 * VARS)
    return (
        new_fields,
        new_velocity,
        grad_fields,
        grad_velocity,
        weights[: 9 * ch].reshape(3, 3, ch, ch)[:, :, :cin],
        weights[cin],
        norm_grads[:, 1],
        norm_grads[:, 0],
        weights[9 * ch : 27 * ch].reshape(2, 3, 3, ch, ch),
        weights[27 * ch : 30 * ch].reshape(3, ch, ch).transpose(1, 0, 2).reshape(ch, 3 * ch),
        weights[30 * ch : 31 * ch],
        weights[31 * ch : 32 * ch, vel],
        weights[cin + 1, vel],
    )


def solution(mesh):
    field = P("batch", None, "lon", None)
    return jax.shard_map(
        partial(on_device, mesh.shape["lon"], mesh.shape["batch"]),
        mesh=mesh,
        in_specs=(
            field,
            field,
            field,
            P("batch", None, "lon"),
            P(None, "lon", None),
            P(),
            P(),
            P(),
            P(),
            P(),
            P(),
            P(),
            P(),
            P(),
            field,
            field,
        ),
        out_specs=(field,) * 4 + (P(),) * 9,
        check_vma=False,
    )
```

time: 2400 us -> 267 us (0.11)
  blocking collectives: 675 us -> 0 us
  local copies, waits for them, and re-layouts: 655 us -> 20.9 us
  matrix products: 475 us -> 0 us
  other arithmetic: 383 us -> 0.7 us
  Pallas kernels: 0 us -> 241 us
  waiting for transfers between devices: 104 us -> 0 us
  starting transfers between devices: 65.4 us -> 0 us
    psum x17 -> x0, blocking collectives: 675 us -> none  [the longest x8 319 us: velocity_back(): lax.psum((grad_first, grad_second), ('lon', 'batch'))]
    dot_general x52 -> x0, matrix products: 309 us -> none  [the longest x8 138 us: attend(): jnp.einsum('abchw,abcwhd->abchd', weights, picked[..., 1, :, :], precisio...]
    pallas_call x0 -> x1, Pallas kernels: none -> 241 us  [on_device(): pl.pallas_call(partial(kernel, (nl, nb, L, W, HEADS)), out_shape=(jax.Sha...]
    conv_general_dilated x36 -> x0, matrix products: 167 us -> none  [conv_same(): lax.conv_general_dilated(padded, kernel, (1, 1), ((1, 1), (0, 0)), dimens...]
    reshape x17 -> x3, local copies, waits for them, and re-layouts: 119 us -> 3.16 us  [the longest x2 3.03 us: state(): x = x.reshape(W, L, ch).transpose(1, 0, 2)[None]]
    another operation x68 -> x0, local copies, waits for them, and re-layouts: 110 us -> none
    scatter-add x4 -> x0, other arithmetic: 94.5 us -> none  [attend(): picked = jnp.take(flat_pairs, flat_index.reshape(-1), axis=1)]
    scatter-add x40 -> x0, local copies, waits for them, and re-layouts: 91 us -> none  [the longest x20 61.5 us: lon_unpad(): return interior.at[:, :, -1].add(beside_all[:, :, 3])]
  transfers between devices with their start and end apart: 81 -> 0, of which waited for: 36 -> 0; matrix products, arithmetic and copies ran while one was open for 14% -> 0% of each run, Pallas kernels for 0% -> 0%
where the time goes in v1:
time: 267 us; the launch traced here: 263 us
  Pallas kernels  241 us (90%)
  local copies, waits for them, and re-layouts  20.9 us (8%)
    pallas_call x1, Pallas kernels, on_device(): pl.pallas_call(partial(kernel, (nl, nb, L, W, HEADS)), out_shape=(jax.Sha...  241 us

profile of v1, /device:TPU:0, one launch (start us, length us, event | category | flops | bytes accessed | tf_op | source)
XLA Modules:
  0.0 263.2 jit_solution(218233267701842641)
XLA Ops:
  0.6 1.0 copy.45
  1.6 1.1 copy.48
  2.6 1.0 copy.49
  3.7 0.7 convert_bitcast_fusion
  4.6 0.9 copy.51
  5.5 1.1 copy.54
  6.7 1.8 concatenate.6
  8.5 0.8 copy.55
  9.4 0.6 concatenate.7.small_ref
  10.1 0.7 pad.9.head_ref
  10.8 240.8 %shard_map.255 = (f32[512,128]{1,0:T(8,128)}, f32[512,128]{1,0:T(8,128)}, f32[4096,128]{1,0:T(8,128)}, f32[2,2,128]{2,1,0:T(2,128)}) custom-call(f32[512,256]{1,0:T(8,128)} %bitcast.34, s32[512,8]{1,0:T(8,128)} %bitcast.41, f32[8,128]{1,0:T(8,128)} %concatenate.7.small_ref, f32[3,3,100,128]{3,2,1,0:T(8,128)} %lift_ref.1, f32[2,3,3,128,128]{4,3,2,1,0:T(8,128)} %conv_ref.1, ...), custom_call_target="tpu_custom_call" | custom-call | tf_op jit(solution)/shard_map/pallas_call | solution.py:913
  251.6 1.6 copy.57
  253.2 0.6 slice.56
  253.8 0.6 slice.57
  254.5 1.4 copy.58
  255.9 0.6 slice.58
  256.5 0.6 slice.59
  257.2 0.8 slice.60
  258.6 0.6 fusion
  259.1 1.1 slice.51
  260.4 0.8 copy.60
  261.2 0.6 slice.53
  261.9 0.7 copy.61
  262.6 0.6 slice_bitcast_fusion
  (27 shorter events, 1.2 us)
Async XLA Ops:
  6.6 1.9 copy-start.1
  6.6 2.7 %copy-start.7 = (f32[10]{0:T(128)S(1)}, f32[10]{0:T(128)}, u32[]{:S(2)}) copy-start(f32[10]{0:T(128)} %param.29) | copy-start | bytes 124
  6.6 2.8 %copy-start.4 = (f32[2,128]{1,0:T(2,128)S(1)}, f32[2,128]{1,0:T(2,128)}, u32[]{:S(2)}) copy-start(f32[2,128]{1,0:T(2,128)} %param.23) | copy-start | bytes 3076
  6.6 2.7 %copy-start.5 = (f32[2,128]{1,0:T(2,128)S(1)}, f32[2,128]{1,0:T(2,128)}, u32[]{:S(2)}) copy-start(f32[2,128]{1,0:T(2,128)} %param.24) | copy-start | bytes 3076
  6.6 2.7 %copy-start.6 = (f32[128]{0:T(128)S(1)}, f32[128]{0:T(128)}, u32[]{:S(2)}) copy-start(f32[128]{0:T(128)} %param.22) | copy-start | bytes 1540
  6.7 3.3 %copy-start.2 = (f32[128,10]{0,1:T(8,128)S(1)}, f32[128,10]{0,1:T(8,128)}, u32[]{:S(2)}) copy-start(f32[128,10]{0,1:T(8,128)} %param.28) | copy-start | bytes 15364
  251.6 5.6 %copy-start = (f32[4096,128]{1,0:T(8,128)S(1)}, f32[4096,128]{1,0:T(8,128)}, u32[]{:S(2)}) copy-start(f32[4096,128]{1,0:T(8,128)} %get-tuple-element.19) | copy-start | bytes 6291460
  253.2 5.4 %copy-start.3 = (f32[2,2,128]{2,1,0:T(2,128)S(1)}, f32[2,2,128]{2,1,0:T(2,128)}, u32[]{:S(2)}) copy-start(f32[2,2,128]{2,1,0:T(2,128)} %get-tuple-element.20) | copy-start | bytes 6148

commit v2 on v1

--- a/solution.py
+++ b/solution.py
@@ -45,18 +45,23 @@
 
 def kernel(
     sizes,
-    start_ref,
-    window_ref,
-    small_ref,
-    lift_ref,
-    conv_ref,
-    qkv_ref,
-    out_ref,
-    head_ref,
-    new_ref,
-    grad_ref,
-    weights_out,
-    norm_out,
+    fields_in,
+    velocity_in,
+    cot_fields_in,
+    cot_velocity_in,
+    masks_in,
+    context_in,
+    window_in,
+    lift_in,
+    conv_in,
+    qkv_in,
+    out_in,
+    head_in,
+    lift_bias_ref,
+    head_bias_ref,
+    gain_ref,
+    shift_ref,
+    all_out,
     ys,
     xh,
     xl,
@@ -99,9 +104,10 @@
     blend,
     dbh,
     dbl,
-    dq,
-    dkv,
+    dqkv,
     dh2,
+    h2,
+    count,
     de1,
     de0,
     sb,
@@ -110,6 +116,18 @@
     rsb,
     norm_acc,
     bias_acc,
+    planes,
+    mask_plane,
+    context_ref,
+    window_ref,
+    lift_ref,
+    conv_ref,
+    qkv_ref,
+    out_ref,
+    head_ref,
+    head_bias_row,
+    grad_ref,
+    load_sems,
     ar_src,
     ar_buf,
     ar_send,
@@ -137,6 +155,8 @@
         t = lax.rem(me + k, nd)
         return (t // nb, lax.rem(t, nb))
 
+    low_half = 1 - me_b // max(nb // 2, 1) if nb > 1 else 0
+    lon_order = sorted(range(nl), key=lambda hop: -min(hop, nl - hop))
     barrier = pltpu.get_barrier_semaphore()
 
     def greet(k, c):
@@ -150,17 +170,23 @@
         ar_buf[a, me] = vals
 
         def send(k, c):
-            pltpu.make_async_remote_copy(
-                ar_src.at[a],
-                ar_buf.at[a, me],
-                ar_send.at[a],
-                ar_recv.at[a],
-                device_id=peer(k),
-                device_id_type=MESH,
-            ).start()
+            to_b = k + low_half * (nb - 1 - 2 * k)
+            for hop in lon_order:
+                copy = pltpu.make_async_remote_copy(
+                    ar_src.at[a],
+                    ar_buf.at[a, me],
+                    ar_send.at[a],
+                    ar_recv.at[a],
+                    device_id=(lax.rem(me_l + hop, nl), to_b),
+                    device_id_type=MESH,
+                )
+                if hop == 0:
+                    pl.when(to_b != me_b)(copy.start)
+                else:
+                    copy.start()
             return c
 
-        lax.fori_loop(1, nd, send, 0)
+        lax.fori_loop(0, nb, send, 0)
 
     def sum_wait(a):
         got = ar_buf.at[a, pl.ds(0, nd - 1)]
@@ -259,23 +285,56 @@
     qkv_base = 27 * ch
     out_base, head_base = 30 * ch, 31 * ch
 
-    ys[0, 2 * L : 2 * L + R] = start_ref[:, :ch]
-    cot = start_ref[:, ch:]
-    for s, weight in enumerate((1.0, 2.0, 2.0, 1.0)):
-        gk[s] = cot * (weight * step_size / 6.0)
-    grad_ref[...] = cot
-    acc[...] = jnp.zeros_like(acc)
-    gw[...] = jnp.zeros_like(gw)
-    norm_acc[...] = jnp.zeros_like(norm_acc)
-    bias_acc[...] = jnp.zeros_like(bias_acc)
+    at_f, at_v, at_cf, at_cv, at_m = (
+        k * VARS for k in (0, 1, 3, 4, 6)
+    )
+    loads = [
+        (fields_in, planes.at[at_f * W : at_v * W]),
+        (velocity_in, planes.at[at_v * W : at_cf * W]),
+        (cot_fields_in, planes.at[at_cf * W : at_cv * W]),
+        (cot_velocity_in, planes.at[at_cv * W : at_m * W]),
+        (masks_in, mask_plane),
+        (context_in, context_ref),
+        (lift_in, lift_ref),
+        (conv_in, conv_ref),
+        (qkv_in, qkv_ref),
+        (out_in, out_ref),
+        (head_in, head_ref),
+        (window_in, window_ref),
+    ]
+    loads = [
+        pltpu.make_async_copy(src, dst, load_sems.at[k])
+        for k, (src, dst) in enumerate(loads)
+    ]
+    for load in loads:
+        load.start()
+    planes[(at_m + 1) * W :] = jnp.zeros((W, L), f32)
+    for load in loads[:6]:
+        load.wait()
+    planes[at_m * W : (at_m + 1) * W] = mask_plane[...].astype(f32)
+    cots = []
+    masks_own = []
+    for col in range(W):
+        at = 2 * L + col * L
+        x = planes[pl.ds(col, at_m + 2, stride=W), :].T
+        ys[0, at : at + L] = jnp.zeros((L, ch), f32)
+        for k in range(3):
+            ys[0, at : at + L, k * VARS : (k + 1) * VARS] = x[:, at_f:at_v]
+            gk[0, at - 2 * L : at - L, k * VARS : (k + 1) * VARS] = x[:, at_cf:at_cv]
+        ys[0, at : at + L, 3 * VARS : 5 * VARS] = x[:, at_v:at_cf]
+        gk[0, at - 2 * L : at - L, 3 * VARS : 5 * VARS] = x[:, at_cv:at_m]
+        gk[0, at - 2 * L : at - L, 5 * VARS :] = jnp.zeros((L, ch - 5 * VARS), f32)
+        ys[0, at : at + L, 5 * VARS : 5 * VARS + context_ref.shape[1]] = context_ref[
+            pl.ds(col, L, stride=W), :
+        ]
+        ys[0, at : at + L, MASK_LANE:] = x[:, at_m : at_m + 1]
+    cot = gk[0]
     mask_own = jnp.broadcast_to(
-        start_ref[:, MASK_LANE : MASK_LANE + 1], (R, LANES)
+        ys[0, 2 * L : 2 * L + R, MASK_LANE : MASK_LANE + 1], (R, LANES)
     )
     count_part = jnp.sum(mask_own, axis=0, keepdims=True)
-
-    pl.semaphore_wait(barrier, nd - 1)
-    halo_start(0, ys, 0, 2)
-    sum_start(4 * SECTIONS, jnp.concatenate([count_part, count_part], axis=0))
+    for load in loads[6:8]:
+        load.wait()
 
     tap[...] = jnp.zeros_like(tap)
     for b in range(3):
@@ -295,6 +354,10 @@
                     at = (p * 3 + i) * ch
                     w3t[b, at : at + ch, j * ch : (j + 1) * ch] = part
 
+    pl.semaphore_wait(barrier, nd - 1)
+    halo_start(0, ys, 0, 2)
+    sum_start(4 * SECTIONS, jnp.concatenate([count_part, count_part], axis=0))
+
     def put_three(target, w):
         n = w.shape[0]
         hi, lo = split(w)
@@ -302,25 +365,41 @@
         target[n : 2 * n] = hi
         target[2 * n :] = lo
 
+    for load in loads[8:]:
+        load.wait()
     put_three(wq3, qkv_ref[...])
     put_three(wqt3, qkv_ref[...].T)
     put_three(wo3, out_ref[...])
     put_three(wot3, out_ref[...].T)
-    put_three(wh3, head_ref[...])
-    put_three(wht3, head_ref[...].T)
-
-    counted = jnp.zeros((R, LANES), f32)
-    key_of = lane_of(R)
-    for k in range(window_ref.shape[1]):
-        entry = jnp.broadcast_to(window_ref[:, k : k + 1], (R, LANES))
-        counted = counted + jnp.where(entry == key_of, 1.0, 0.0)
-    mult[...] = counted.reshape(W, L, LANES)
-    for s in range(SECTIONS):
-        for ref in (kh, kl, vh, vl):
-            ref[s, R1:] = jnp.zeros((L, ch), bf16)
-
-    head_rows = lax.broadcasted_iota(jnp.int32, (HEADS * L, ch), 0) // L
-    head_lanes = lax.broadcasted_iota(jnp.int32, (HEADS * L, ch), 1) // (ch // HEADS)
+    tap[...] = jnp.zeros_like(tap)
+    tap[3 * VARS : 5 * VARS] = head_ref[...]
+    put_three(wht3, tap[...])
+    put_three(wh3, tap[...].T)
+    head_bias_row[...] = jnp.zeros_like(head_bias_row)
+    head_bias_row[:, 3 * VARS : 5 * VARS] = head_bias_ref[...]
+    for s, weight in enumerate((1.0, 2.0, 2.0, 1.0)):
+        gk[s] = cot * (weight * step_size / 6.0)
+    grad_ref[...] = cot
+    acc[...] = jnp.zeros_like(acc)
+    gw[...] = jnp.zeros_like(gw)
+    norm_acc[...] = jnp.zeros_like(norm_acc)
+    bias_acc[...] = jnp.zeros_like(bias_acc)
+
+    pair = 2 * L
+    shape = (2 * pair, HEADS * pair)
+    key_of = lax.broadcasted_iota(jnp.int32, shape, 0)
+    key_of = key_of - lax.broadcasted_iota(jnp.int32, shape, 1) // L % 2 * L
+    for p in range(W // 2):
+        entries = lanes_cat(*[window_ref[2 * p], window_ref[2 * p + 1]] * HEADS)
+        counted = jnp.zeros(shape, f32)
+        for k in range(entries.shape[0]):
+            counted = counted + jnp.where(entries[k : k + 1] == key_of, 1.0, 0.0)
+        mult[p] = jnp.where(
+            counted > 0.0, jnp.log(jnp.maximum(counted, 1.0)), -1e30
+        )
+
+    head_rows = lax.broadcasted_iota(jnp.int32, (HEADS * pair, ch), 0) // pair
+    head_lanes = lax.broadcasted_iota(jnp.int32, (HEADS * pair, ch), 1) // (ch // HEADS)
     head_mask = jnp.where(head_rows == head_lanes, 1.0, 0.0)
     head_mask_h = head_mask.astype(bf16)
     scale = (ch // HEADS) ** -0.5
@@ -330,15 +409,12 @@
 
     def heads_sum(x):
         x = x * head_mask
-        return sum(x[h * L : (h + 1) * L] for h in range(1, HEADS)) + x[:L]
-
-    total_count = sum_wait(4 * SECTIONS)[0:1]
-    inverse_count = 1.0 / total_count
-
-    lift_bias = small_ref[0:1]
-    head_bias = small_ref[1:2]
-    gains = [small_ref[2:3], small_ref[3:4]]
-    shifts = [small_ref[4:5], small_ref[5:6]]
+        return sum(x[h * pair : (h + 1) * pair] for h in range(1, HEADS)) + x[:pair]
+
+    lift_bias = lift_bias_ref[...]
+    head_bias = head_bias_row[...]
+    gains = [gain_ref[0:1], gain_ref[1:2]]
+    shifts = [shift_ref[0:1], shift_ref[1:2]]
 
     def stats(h):
         weighted = h * mask[2 * L : 2 * L + R]
@@ -351,6 +427,7 @@
         )
 
     def normalise(s, b, sums):
+        total_count = count[0:1]
         average = sums[0:1] / total_count
         spread = sums[1:2] / total_count - average * average
         inverse = lax.rsqrt(spread + epsilon)
@@ -366,14 +443,10 @@
         )
         return z * below, slope
 
-    group = 4
+    group = 2
 
     def forward(s, carry):
         hb = s * 6
-
-        @pl.when(s > 0)
-        def _():
-            halo_start(hb, ys, s, 2)
 
         halo_wait(hb, ys, s, 2)
 
@@ -394,6 +467,10 @@
         hi, lo = split(x)
         xh[s] = hi
         xl[s] = lo
+        first = conv(xh.at[s], xl.at[s], 0, R, w3f[0]) + lift_bias
+        h0[s, 2 * L : 2 * L + R] = first
+        sum_start(s * 4, stats(first))
+        halo_start(hb + 1, h0, s, 2)
         flux = y1 * lroll(y1, -3 * VARS)
         flux = jnp.where(lane < 2 * VARS, flux, 0.0)
         own_lane = lane_of(R)
@@ -404,10 +481,11 @@
         t = -(t_lat + lroll(t_lon, -VARS))
         tend[...] = t + lroll(t, VARS) + lroll(t, 2 * VARS)
 
-        first = conv(xh.at[s], xl.at[s], 0, R, w3f[0]) + lift_bias
-        h0[s, 2 * L : 2 * L + R] = first
-        sum_start(s * 4, stats(first))
-        halo_start(hb + 1, h0, s, 2)
+
+        @pl.when(s == 0)
+        def _():
+            count[...] = sum_wait(4 * SECTIONS)
+
         average, inverse = normalise(s, 0, sum_wait(s * 4))
         halo_wait(hb + 1, h0, s, 2)
         act, slope = activity(h0[s, L : L + R1], 0, average, inverse)
@@ -427,6 +505,7 @@
         a2h[s] = hi
         a2l[s] = lo
         third = h1[s, L : L + R1] + conv(a2h.at[s], a2l.at[s], 0, R1, w3f[2])
+        h2[...] = third
         hi, lo = split(third)
         h2h[s] = hi
         h2l[s] = lo
@@ -435,74 +514,98 @@
         qh[s] = hi
         ql[s] = lo
         hi, lo = split(mixing[:, ch : 2 * ch])
-        kh[s, :R1] = hi
-        kl[s, :R1] = lo
+        kh[s] = hi
+        kl[s] = lo
         hi, lo = split(mixing[:, 2 * ch :])
-        vh[s, :R1] = hi
-        vl[s, :R1] = lo
-
-        def attend(g, c):
-            cols = [g * group + k for k in range(group)]
+        vh[s] = hi
+        vl[s] = lo
+
+        def attend(pairs):
             scores = []
-            for col in cols:
-                at = pl.multiple_of(col * L, L)
-                q_h = per_head(qh[s, pl.ds(at, L)])
-                q_l = per_head(ql[s, pl.ds(at, L)])
-                k_h = kh[s, pl.ds(at, 4 * L)]
-                k_l = kl[s, pl.ds(at, 4 * L)]
+            for p in pairs:
+                at = pl.multiple_of(p * pair, pair)
+                q_h = per_head(qh[s, pl.ds(at, pair)])
+                q_l = per_head(ql[s, pl.ds(at, pair)])
+                k_h = kh[s, pl.ds(at, 2 * pair)]
+                k_l = kl[s, pl.ds(at, 2 * pair)]
                 scores.append(
                     dot(
-                        lanes_cat(q_h, q_l, q_h),
-                        lanes_cat(k_h, k_h, k_l),
+                        lanes_cat(k_h, k_l, k_h),
+                        lanes_cat(q_h, q_h, q_l),
                         ((1,), (1,)),
                     )
                 )
             weights = []
-            for col, score in zip(cols, scores):
-                m = jnp.concatenate([mult[col]] * HEADS, axis=0)
-                score = jnp.where(m > 0.0, score, -1e30)
-                top = jnp.max(score, axis=1, keepdims=True)
-                e = m * jnp.exp(score - top)
-                p = e / jnp.sum(e, axis=1, keepdims=True)
-                probs[s, col] = p
-                weights.append(p)
-            for col, p in zip(cols, weights):
-                at = pl.multiple_of(col * L, L)
-                p_h, p_l = split(p)
-                v_h = vh[s, pl.ds(at, 4 * L)]
-                v_l = vl[s, pl.ds(at, 4 * L)]
+            for p, score in zip(pairs, scores):
+                score = score + mult[p]
+                e = jnp.exp(score - jnp.max(score, axis=0, keepdims=True))
+                e = e * (1.0 / jnp.sum(e, axis=0, keepdims=True))
+                probs[s, p] = e
+                weights.append(e)
+            for p, e in zip(pairs, weights):
+                at = pl.multiple_of(p * pair, pair)
+                p_h, p_l = split(e.T)
+                v_h = vh[s, pl.ds(at, 2 * pair)]
+                v_l = vl[s, pl.ds(at, 2 * pair)]
                 o = dot(
                     lanes_cat(p_h, p_l, p_h),
                     jnp.concatenate([v_h, v_h, v_l], axis=0),
                 )
-                blend[pl.ds(at, L)] = heads_sum(o)
-            return c
-
-        lax.fori_loop(0, W // group, attend, 0)
-        hi, lo = split(blend[...])
-        bh[s] = hi
-        bl[s] = lo
-        fourth = third[L : L + R] + dot(lanes_cat(hi, lo, hi), wo3[...])
-        hi, lo = split(fourth)
-        h3h[s] = hi
-        h3l[s] = lo
-        slope_now = (
-            tend[...] + dot(lanes_cat(hi, lo, hi), wh3[...]) + head_bias
-        )
+                blend[pl.ds(at, pair)] = heads_sum(o)
+
         weight = jnp.where((s == 0) | (s == SECTIONS - 1), 1.0, 2.0)
-        acc[...] += weight * slope_now
+        factor = jnp.where(s == SECTIONS - 2, 1.0, 0.5) * step_size
+
+        def finish(ranges):
+            def take(ref, base=0):
+                return jnp.concatenate(
+                    [ref[base + a : base + b] for a, b in ranges], axis=0
+                )
+
+            def give(ref, value, base=0):
+                at = 0
+                for a, b in ranges:
+                    ref[base + a : base + b] = value[at : at + b - a]
+                    at += b - a
+
+            hi, lo = split(take(blend))
+            give(bh.at[s], hi)
+            give(bl.at[s], lo)
+            fourth = take(h2, L) + dot(lanes_cat(hi, lo, hi), wo3[...])
+            hi, lo = split(fourth)
+            give(h3h.at[s], hi)
+            give(h3l.at[s], lo)
+            slope_now = (
+                take(tend) + dot(lanes_cat(hi, lo, hi), wh3[...]) + head_bias
+            )
+            give(acc, take(acc) + weight * slope_now)
+
+            @pl.when(s < SECTIONS - 1)
+            def _():
+                give(
+                    ys.at[s + 1],
+                    take(ys.at[0], 2 * L) + factor * slope_now,
+                    2 * L,
+                )
+
+        last = W // 2 - 1
+        attend([0, last])
+        finish([(0, pair), (R - pair, R)])
 
         @pl.when(s < SECTIONS - 1)
         def _():
-            factor = jnp.where(s == SECTIONS - 2, 1.0, 0.5) * step_size
-            ys[s + 1, 2 * L : 2 * L + R] = (
-                ys[0, 2 * L : 2 * L + R] + factor * slope_now
-            )
-
+            halo_start(hb + 6, ys, s + 1, 2)
+
+        def inner(k, c):
+            attend([1 + group * k + m for m in range(group)])
+            return c
+
+        lax.fori_loop(0, (last - 1) // group, inner, 0)
+        finish([(pair, R - pair)])
         return carry
 
     lax.fori_loop(0, SECTIONS, forward, 0)
-    new_ref[...] = ys[0, 2 * L : 2 * L + R] + (step_size / 6.0) * acc[...]
+    acc[...] = ys[0, 2 * L : 2 * L + R] + (step_size / 6.0) * acc[...]
 
     def norm_back(s, b, h, grad_act, slope, through):
         average = norms[s, b, 0:1]
@@ -524,7 +627,7 @@
         hat = (h - average) * inverse
         norm_acc[b] += sums
         return direct - weight_mask * (
-            gains[b] * inverse * inverse_count
+            gains[b] * inverse / count[0:1]
         ) * (sums[0:1] + hat * sums[1:2])
 
     def backward(turn, carry):
@@ -533,97 +636,107 @@
         g = gk[s]
         g_h, g_l = split(g)
         grad3 = dot(lanes_cat(g_h, g_l, g_h), wht3[...])
-        bias_acc[1:2] += jnp.sum(g, axis=0, keepdims=True)
-        gw[head_base : head_base + ch] += rows_product(h3h[s], h3l[s], g_h, g_l)
-        hi, lo = split(grad3)
-        gw[out_base : out_base + ch] += rows_product(bh[s], bl[s], hi, lo)
-        hi, lo = split(dot(lanes_cat(hi, lo, hi), wot3[...]))
+        grad3_h, grad3_l = split(grad3)
+        hi, lo = split(dot(lanes_cat(grad3_h, grad3_l, grad3_h), wot3[...]))
         dbh[...] = hi
         dbl[...] = lo
-        dkv[...] = jnp.zeros_like(dkv)
-
-        def attend_back(gi, c):
-            cols = [gi * group + k for k in range(group)]
+        dqkv[...] = jnp.zeros_like(dqkv)
+
+        def attend_back(pairs):
             dps = []
-            for col in cols:
-                at = pl.multiple_of(col * L, L)
-                d_h = per_head(dbh[pl.ds(at, L)])
-                d_l = per_head(dbl[pl.ds(at, L)])
-                v_h = vh[s, pl.ds(at, 4 * L)]
-                v_l = vl[s, pl.ds(at, 4 * L)]
+            for p in pairs:
+                at = pl.multiple_of(p * pair, pair)
+                d_h = per_head(dbh[pl.ds(at, pair)])
+                d_l = per_head(dbl[pl.ds(at, pair)])
+                v_h = vh[s, pl.ds(at, 2 * pair)]
+                v_l = vl[s, pl.ds(at, 2 * pair)]
                 dps.append(
                     dot(
-                        lanes_cat(d_h, d_l, d_h),
-                        lanes_cat(v_h, v_h, v_l),
+                        lanes_cat(v_h, v_l, v_h),
+                        lanes_cat(d_h, d_h, d_l),
                         ((1,), (1,)),
                     )
                 )
             dss = []
-            for col, dp in zip(cols, dps):
-                p = probs[s, col]
-                mean = jnp.sum(p * dp, axis=1, keepdims=True)
-                dss.append(p * (dp - mean))
-            for col, ds in zip(cols, dss):
-                at = pl.multiple_of(col * L, L)
-                ds_h, ds_l = split(ds)
-                k_h = kh[s, pl.ds(at, 4 * L)]
-                k_l = kl[s, pl.ds(at, 4 * L)]
+            for p, dp in zip(pairs, dps):
+                e = probs[s, p]
+                dss.append(e * (dp - jnp.sum(e * dp, axis=0, keepdims=True)))
+            for p, ds in zip(pairs, dss):
+                at = pl.multiple_of(p * pair, pair)
+                k_h = kh[s, pl.ds(at, 2 * pair)]
+                k_l = kl[s, pl.ds(at, 2 * pair)]
+                t_h, t_l = split(ds.T)
                 o = dot(
-                    lanes_cat(ds_h, ds_l, ds_h),
+                    lanes_cat(t_h, t_l, t_h),
                     jnp.concatenate([k_h, k_h, k_l], axis=0),
                 )
-                dq[pl.ds(at, L)] = heads_sum(o) * scale
-                q_h = per_head(qh[s, pl.ds(at, L)])
-                q_l = per_head(ql[s, pl.ds(at, L)])
-                t_h, t_l = split(ds.T)
-                dkv[pl.ds(at, 4 * L), :ch] += dot(
-                    lanes_cat(t_h, t_l, t_h),
-                    jnp.concatenate([q_h, q_h, q_l], axis=0),
-                )
-                t_h, t_l = split(probs[s, col].T)
-                d_h = per_head(dbh[pl.ds(at, L)])
-                d_l = per_head(dbl[pl.ds(at, L)])
-                dkv[pl.ds(at, 4 * L), ch:] += dot(
-                    lanes_cat(t_h, t_l, t_h),
-                    jnp.concatenate([d_h, d_h, d_l], axis=0),
-                )
-            return c
-
-        lax.fori_loop(0, W // group, attend_back, 0)
+                dqkv[pl.ds(at + L, pair), :ch] = heads_sum(o) * scale
+                q_h = per_head(qh[s, pl.ds(at, pair)])
+                q_l = per_head(ql[s, pl.ds(at, pair)])
+                s_h, s_l = split(ds)
+                o = dot(s_h, lanes_cat(q_h, q_l))
+                o = o[:, :ch] + o[:, ch:] + dot(s_l, q_h)
+                dqkv[pl.ds(at, 2 * pair), ch : 2 * ch] += o
+                d_h = per_head(dbh[pl.ds(at, pair)])
+                d_l = per_head(dbl[pl.ds(at, pair)])
+                s_h, s_l = split(probs[s, p])
+                o = dot(s_h, lanes_cat(d_h, d_l))
+                o = o[:, :ch] + o[:, ch:] + dot(s_l, d_h)
+                dqkv[pl.ds(at, 2 * pair), 2 * ch :] += o
+
+        last = W // 2 - 1
+        attend_back([0, last])
+        edge_h, edge_l = split(
+            jnp.concatenate([dqkv[:pair], dqkv[R1 - pair :]], axis=0)
+        )
+        part = dot(lanes_cat(edge_h, edge_l, edge_h), wqt3[...])
         zeros = jnp.zeros((L, ch), f32)
-        d_all = lanes_cat(
-            jnp.concatenate([zeros, dq[...], zeros], axis=0), dkv[:R1]
-        )
-        d_h, d_l = split(d_all)
-        part = dot(lanes_cat(d_h, d_l, d_h), wqt3[...])
-        dh2[...] = part + jnp.concatenate([zeros, grad3, zeros], axis=0)
-        sb[s, 0, : 2 * L] = dh2[: 2 * L]
-        sb[s, 0, 2 * L :] = gk[s, :L]
-        sb[s, 1, : 2 * L] = dh2[R:]
-        sb[s, 1, 2 * L :] = gk[s, R - L :]
+        part = part + jnp.concatenate(
+            [zeros, grad3[:L], grad3[R - L :], zeros], axis=0
+        )
+        dh2[:pair] = part[:pair]
+        dh2[R1 - pair :] = part[pair:]
+        sb[s, 0, :pair] = part[:pair]
+        sb[s, 0, pair:] = gk[s, :L]
+        sb[s, 1, :pair] = part[pair:]
+        sb[s, 1, pair:] = gk[s, R - L :]
         edges = [
             side_copy(hb + 3, side, sb.at[s, side], rb.at[s, side])
             for side in range(2)
         ]
         for e in edges:
             e.start()
+
+        def inner(k, c):
+            attend_back([1 + group * k + m for m in range(group)])
+            return c
+
+        lax.fori_loop(0, (last - 1) // group, inner, 0)
+        d_h, d_l = split(dqkv[...])
+        mid_h, mid_l = d_h[pair : R1 - pair], d_l[pair : R1 - pair]
+        dh2[pair : R1 - pair] = grad3[L : R - L] + dot(
+            lanes_cat(mid_h, mid_l, mid_h), wqt3[...]
+        )
+        for e in edges:
+            e.wait()
+        dh2[:pair] += rb[s, 1, :pair]
+        dh2[R1 - pair :] += rb[s, 0, :pair]
+
+        t_h, t_l = lat_triple(dh2[...])
+        grad_act = conv_back(t_h, t_l, R, w3t[2])
+        sums, direct = norm_back(
+            s, 1, h1[s, 2 * L : 2 * L + R], grad_act, dg2[s], dh2[L : L + R]
+        )
+        sum_start(s * 4 + 2, sums)
+        de1[s, 2 * L : 2 * L + R] = direct
+        halo_start(hb + 4, de1, s, 1)
+        bias_acc[1:2] += jnp.sum(g, axis=0, keepdims=True)
+        gw[head_base : head_base + ch] += rows_product(h3h[s], h3l[s], g_h, g_l)
+        gw[out_base : out_base + ch] += rows_product(bh[s], bl[s], grad3_h, grad3_l)
         wide = rows_product(h2h[s], h2l[s], d_h, d_l)
         for k in range(3):
             at = qkv_base + k * ch
             gw[at : at + ch] += wide[:, k * ch : (k + 1) * ch]
-        for e in edges:
-            e.wait()
-        dh2[: 2 * L] += rb[s, 1, : 2 * L]
-        dh2[R:] += rb[s, 0, : 2 * L]
-
-        t_h, t_l = lat_triple(dh2[...])
-        grad_act = conv_back(t_h, t_l, R, w3t[2])
-        sums, direct = norm_back(
-            s, 1, h1[s, 2 * L : 2 * L + R], grad_act, dg2[s], dh2[L : L + R]
-        )
-        sum_start(s * 4 + 2, sums)
-        de1[s, 2 * L : 2 * L + R] = direct
-        halo_start(hb + 4, de1, s, 1)
         add_conv_grad(
             conv_base + 9 * ch,
             a2h[s, L : L + R1],
@@ -701,7 +814,26 @@
 
     gw[ch - 28 : ch - 27] = bias_acc[0:1]
     gw[ch - 27 : ch - 26] = bias_acc[1:2]
-    norm_out[...] = norm_acc[...]
+    weights_out = all_out.at[: gw.shape[0]]
+    all_out[gw.shape[0] : gw.shape[0] + 4] = norm_acc[...].reshape(4, ch)
+    lane = lane_of(R)
+    new, grad = acc[...], grad_ref[...]
+    merged = jnp.where(
+        lane < at_v,
+        new,
+        jnp.where(
+            lane < at_cf,
+            lroll(new, at_v - 3 * VARS),
+            jnp.where(
+                lane < at_cv, lroll(grad, at_cf), lroll(grad, at_cv - 3 * VARS)
+            ),
+        ),
+    )
+    for col in range(W):
+        x = merged[col * L : (col + 1) * L].T
+        all_out[pl.ds(gw.shape[0] + 8 + col, at_m, stride=W), :] = lanes_cat(
+            x[:at_m], jnp.zeros((at_m, ch - L), f32)
+        )
 
     stages = []
     step = 1
@@ -781,6 +913,36 @@
         pltpu.make_async_copy(got, got, ag_send.at[t]).wait()
 
 
+def hand_out(rows, weights, *outs):
+    fields = outs[:4]
+    lift, lift_bias, gain, shift, conv, qkv, out, head, head_bias = outs[4:]
+    ch = LANES
+    at = rows + 8
+    for ref in fields:
+        ref[...] = weights[at : at + ref.shape[0], : ref.shape[1]]
+        at += ref.shape[0]
+    cin = lift.shape[2]
+    vel = slice(3 * VARS, 5 * VARS)
+    for i in range(3):
+        for j in range(3):
+            at = (i * 3 + j) * ch
+            lift[i, j] = weights[at : at + cin]
+            for b in range(2):
+                at_conv = at + (b + 1) * 9 * ch
+                conv[b, i, j] = weights[at_conv : at_conv + ch]
+    lift_bias[...] = weights[cin : cin + 1]
+    head_bias[...] = weights[cin + 1 : cin + 2, vel]
+    for b in range(2):
+        at = rows + 2 * b
+        shift[b : b + 1] = weights[at : at + 1]
+        gain[b : b + 1] = weights[at + 1 : at + 2]
+    for k in range(3):
+        at = (27 + k) * ch
+        qkv[:, k * ch : (k + 1) * ch] = weights[at : at + ch]
+    out[...] = weights[30 * ch : 31 * ch]
+    head[...] = weights[31 * ch : 32 * ch].T[vel]
+
+
 def on_device(
     nl,
     nb,
@@ -805,39 +967,10 @@
     R, R1, R2 = L * W, L * (W + 2), L * (W + 4)
     ch = LANES
     nd = nl * nb
-    grid = (L, W)
-    used = 3 * VARS + 2 * VARS + context.shape[-1]
-    start = jnp.concatenate(
-        [
-            fields[0],
-            fields[0],
-            fields[0],
-            velocity[0],
-            context[0],
-            jnp.zeros((*grid, MASK_LANE - used), f32),
-            masks[0].astype(f32)[..., None],
-            cot_fields[0],
-            cot_fields[0],
-            cot_fields[0],
-            cot_velocity[0],
-            jnp.zeros((*grid, ch - 5 * VARS), f32),
-        ],
-        axis=-1,
-    )
-    start = start.transpose(1, 0, 2).reshape(R, 2 * ch)
-    keys = window.transpose(1, 0, 2).reshape(R, window.shape[-1])
-    side = ((0, 0), (3 * VARS, ch - 5 * VARS))
-    small = jnp.concatenate(
-        [
-            lift_bias[None],
-            jnp.pad(head_bias[None], side),
-            norm_gain,
-            norm_shift,
-            jnp.zeros((2, ch), f32),
-        ],
-        axis=0,
-    )
-    head = jnp.pad(head_weight, side)
+
+    def flat(x):
+        return x[0].transpose(2, 1, 0).reshape(-1, L)
+
     S = SECTIONS
     rows = 32 * ch
     rows = -(-rows // (8 * nd)) * 8 * nd
@@ -860,11 +993,11 @@
         vm((S, R1, ch), bf16),
         vm((S, R, ch), bf16),
         vm((S, R, ch), bf16),
-        vm((S, R1 + L, ch), bf16),
-        vm((S, R1 + L, ch), bf16),
-        vm((S, R1 + L, ch), bf16),
-        vm((S, R1 + L, ch), bf16),
-        vm((S, W, HEADS * L, ch), f32),
+        vm((S, R1, ch), bf16),
+        vm((S, R1, ch), bf16),
+        vm((S, R1, ch), bf16),
+        vm((S, R1, ch), bf16),
+        vm((S, W // 2, 4 * L, 2 * HEADS * L), f32),
         vm((S, R, ch), bf16),
         vm((S, R, ch), bf16),
         vm((S, R, ch), bf16),
@@ -874,7 +1007,7 @@
         vm((R, ch), f32),
         vm((R, ch), f32),
         vm((R2, ch), f32),
-        vm((W, L, ch), f32),
+        vm((W // 2, 4 * L, 2 * HEADS * L), f32),
         vm((3, 9 * ch, 3 * ch), bf16),
         vm((3, 9 * ch, 3 * ch), bf16),
         vm((3 * ch, 3 * ch), bf16),
@@ -887,9 +1020,10 @@
         vm((R, ch), f32),
         vm((R, ch), bf16),
         vm((R, ch), bf16),
-        vm((R, ch), f32),
-        vm((R1 + L, 2 * ch), f32),
+        vm((R1, 3 * ch), f32),
         vm((R1, ch), f32),
+        vm((R1, ch), f32),
+        vm((2, ch), f32),
         vm((S, R2, ch), f32),
         vm((S, R2, ch), f32),
         vm((S, 2, 3 * L, ch), f32),
@@ -898,6 +1032,18 @@
         vm((rows, ch), f32),
         vm((2, 2, ch), f32),
         vm((2, ch), f32),
+        vm((32 * W, L), f32),
+        vm((W, L), jnp.int32),
+        vm((R, context.shape[-1]), f32),
+        vm((W, window.shape[-1], L), jnp.int32),
+        vm(lift_weight.shape, f32),
+        vm(conv_weight.shape, f32),
+        vm(attn_qkv.shape, f32),
+        vm(attn_out.shape, f32),
+        vm(head_weight.shape[::-1], f32),
+        vm((1, ch), f32),
+        vm((R, ch), f32),
+        dma((12,)),
         vm((4 * S + 1, 2, ch), f32),
         vm((4 * S + 1, nd, 2, ch), f32),
         dma((4 * S + 1,)),
@@ -910,44 +1056,68 @@
         dma((stage_count,)),
     ]
     whole = pl.BlockSpec(memory_space=pltpu.VMEM)
-    new, grad, weights, norm_grads = pl.pallas_call(
+    apart = pl.BlockSpec(memory_space=pl.ANY)
+    results = pl.pallas_call(
         partial(kernel, (nl, nb, L, W, HEADS)),
-        out_shape=(
-            jax.ShapeDtypeStruct((R, ch), f32),
-            jax.ShapeDtypeStruct((R, ch), f32),
-            jax.ShapeDtypeStruct((rows, ch), f32),
-            jax.ShapeDtypeStruct((2, 2, ch), f32),
-        ),
-        in_specs=[whole] * 8,
-        out_specs=(whole,) * 4,
+        out_shape=jax.ShapeDtypeStruct((rows + 8 + 6 * VARS * W, ch), f32),
+        in_specs=[apart] * 12 + [whole] * 4,
+        out_specs=whole,
         scratch_shapes=scratch,
         compiler_params=pltpu.CompilerParams(
             collective_id=0, has_side_effects=True, vmem_limit_bytes=60 * 2**20
         ),
-    )(start, keys, small, lift_weight, conv_weight, attn_qkv, attn_out, head)
-
-    def state(x):
-        x = x.reshape(W, L, ch).transpose(1, 0, 2)[None]
-        return x[..., :VARS], x[..., 3 * VARS : 5 * VARS]
-
-    new_fields, new_velocity = state(new)
-    grad_fields, grad_velocity = state(grad)
-    cin = lift_weight.shape[2]
-    vel = slice(3 * VARS, 5 * VARS)
+    )(
+        flat(fields),
+        flat(velocity),
+        flat(cot_fields),
+        flat(cot_velocity),
+        masks[0].T,
+        context.reshape(R, -1),
+        window.transpose(1, 2, 0),
+        lift_weight,
+        conv_weight,
+        attn_qkv,
+        attn_out,
+        head_weight.T,
+        lift_bias[None],
+        head_bias[None],
+        norm_gain,
+        norm_shift,
+    )
+    pixels = VARS * W
+    shapes = (
+        (pixels, L),
+        (2 * pixels, L),
+        (pixels, L),
+        (2 * pixels, L),
+        lift_weight.shape,
+        (1, ch),
+        norm_gain.shape,
+        norm_shift.shape,
+        conv_weight.shape,
+        attn_qkv.shape,
+        attn_out.shape,
+        head_weight.shape[::-1],
+        (1, head_bias.shape[0]),
+    )
+    outs = pl.pallas_call(
+        partial(hand_out, rows),
+        out_shape=tuple(jax.ShapeDtypeStruct(shape, f32) for shape in shapes),
+        in_specs=[whole],
+        out_specs=(whole,) * len(shapes),
+        compiler_params=pltpu.CompilerParams(vmem_limit_bytes=32 * 2**20),
+    )(results)
+
+    def field(x):
+        return x.reshape(-1, W, L).transpose(2, 1, 0)[None]
+
     return (
-        new_fields,
-        new_velocity,
-        grad_fields,
-        grad_velocity,
-        weights[: 9 * ch].reshape(3, 3, ch, ch)[:, :, :cin],
-        weights[cin],
-        norm_grads[:, 1],
-        norm_grads[:, 0],
-        weights[9 * ch : 27 * ch].reshape(2, 3, 3, ch, ch),
-        weights[27 * ch : 30 * ch].reshape(3, ch, ch).transpose(1, 0, 2).reshape(ch, 3 * ch),
-        weights[30 * ch : 31 * ch],
-        weights[31 * ch : 32 * ch, vel],
-        weights[cin + 1, vel],
+        *(field(x) for x in outs[:4]),
+        outs[4],
+        outs[5][0],
+        *outs[6:11],
+        outs[11].T,
+        outs[12][0],
     )
 
 

time: 267 us -> 221 us (0.83)
  Pallas kernels: 241 us -> 216 us
  local copies, waits for them, and re-layouts: 20.9 us -> 1.66 us
    pallas_call x1 -> x2, Pallas kernels: 241 us -> 216 us  [the longest x1 214 us: on_device(): pl.pallas_call(partial(kernel, (nl, nb, L, W, HEADS)), out_shape=jax.Shap...]
    squeeze x7 -> x0, local copies, waits for them, and re-layouts: 6.14 us -> none  [the longest x1 1.05 us: on_device(): velocity[0]]
    slice x11 -> x0, local copies, waits for them, and re-layouts: 5.75 us -> none  [the longest x4 2.52 us: state(): return (x[..., :VARS], x[..., 3 * VARS:5 * VARS])]
    reshape x3 -> x0, local copies, waits for them, and re-layouts: 3.16 us -> none  [the longest x2 3.03 us: state(): x = x.reshape(W, L, ch).transpose(1, 0, 2)[None]]
where the time goes in v2:
time: 221 us; the launch traced here: 218 us
  Pallas kernels  216 us (98%)
    pallas_call x1, Pallas kernels, on_device(): pl.pallas_call(partial(kernel, (nl, nb, L, W, HEADS)), out_shape=jax.Shap...  214 us

profile of v2, /device:TPU:0, one launch (start us, length us, event | category | flops | bytes accessed | tf_op | source)
XLA Modules:
  0.0 217.9 jit_solution(10474260851027394199)
XLA Ops:
  0.7 214.2 %shard_map.255.weights = f32[4584,128]{1,0:T(8,128)} custom-call(f32[80,32]{1,0:T(8,128)} %bitcast.55, f32[160,32]{1,0:T(8,128)} %bitcast.52, f32[80,32]{1,0:T(8,128)} %bitcast.56, f32[160,32]{1,0:T(8,128)} %bitcast.53, s32[16,32]{1,0:T(8,128)} %bitcast.57, f32[512,75]{1,0:T(8,128)} %bitcast.51, s32[16,8,32]{2,1,0:T(8,128)} %bitcast.54, ...), custom_call_target="tpu_custom_call" | custom-call | tf_op jit(solution)/shard_map/pallas_call | solution.py:1060
  214.8 0.0 copy-start
  214.9 1.7 copy-done
  216.5 1.4 shard_map.256
Async XLA Ops:
  214.8 1.7 copy-start

commit v3 on v2

--- a/solution.py
+++ b/solution.py
@@ -33,14 +33,34 @@
     return jnp.concatenate(parts, axis=1)
 
 
-def factors(n):
+def factors(n, largest):
     out = []
-    while n > 4 and n % 2 == 0:
+    while n > largest and n % 2 == 0:
         out.append(2)
         n //= 2
     if n > 1:
         out.append(n)
     return out
+
+
+def job_plan(rows, unit):
+    late = -(-9 * LANES // unit)
+    middle = -(-18 * LANES // unit) - late
+    early = rows // unit - late - middle
+    split_late, split_early = (late + 1) // 2, (early + 1) // 2
+    sizes = (
+        (split_late, "A", 0),
+        (late - split_late, "B", 0),
+        (middle, "C", 1),
+        (split_early, "A", 2),
+        (early - split_early, "B", 2),
+    )
+    plan, at = [], 0
+    for units, order, kind in sizes:
+        if units:
+            plan.append((at * unit, units * unit, order, kind))
+        at += units
+    return plan
 
 
 def kernel(
@@ -285,6 +305,147 @@
     qkv_base = 27 * ch
     out_base, head_base = 30 * ch, 31 * ch
 
+    all_rows = gw.shape[0]
+    unit = 8 * nd
+    minor, batch_parts = factors(nl, 2), factors(nb, 4)
+    axes = [("lon", n) for n in minor] + [("batch", n) for n in batch_parts]
+    steps = {"lon": 1, "batch": 1}
+    members = []
+    for axis, n in axes:
+        mine = me_l if axis == "lon" else me_b
+        members.append((axis, steps[axis], n, lax.rem(mine // steps[axis], n)))
+        steps[axis] *= n
+    def stage_of(member):
+        axis, step, n, idx = member
+
+        def device_of(q):
+            shift = (q - idx) * step
+            if axis == "lon":
+                return (me_l + shift, me_b)
+            return (me_l, me_b + shift)
+
+        return n, idx, device_of
+
+    first, rest = members[:1], members[1:]
+    orders = {
+        "A": first + rest,
+        "B": first + rest[1::-1] + rest[2:],
+        "C": first + rest[::-1],
+    }
+
+    def rows_at(at, n):
+        return pl.ds(pl.multiple_of(at, 8), n)
+
+    class Job:
+        def __init__(self, number, base, size, order):
+            self.number = number
+            self.stages = stages = [stage_of(m) for m in orders[order]]
+            self.regions = []
+            off, slot = base, base
+            for n, idx, _ in stages:
+                part = size // n
+                self.regions.append((off, part, slot))
+                off = off + idx * part
+                slot += (n - 1) * part
+                size = part
+            self.own, self.size = off, size
+            self.done, self.todo = 0, list(self.moves())
+
+        def scatter_start(self, t):
+            n, idx, device_of = self.stages[t]
+            off, part, slot = self.regions[t]
+            for k in range(1, n):
+                q = lax.rem(idx + k, n)
+                pltpu.make_async_remote_copy(
+                    gw.at[rows_at(off + q * part, part)],
+                    rsb.at[pl.ds(slot + (n - 1 - k) * part, part)],
+                    rs_send.at[self.number, t],
+                    rs_recv.at[self.number, t],
+                    device_id=device_of(q),
+                    device_id_type=MESH,
+                ).start()
+
+        def scatter_finish(self, t):
+            n, idx, _ = self.stages[t]
+            off, part, slot = self.regions[t]
+            got = rsb.at[pl.ds(slot, (n - 1) * part)]
+            pltpu.make_async_copy(got, got, rs_recv.at[self.number, t]).wait()
+            pltpu.make_async_copy(got, got, rs_send.at[self.number, t]).wait()
+            mine = off + idx * part
+            chunk = math.gcd(part, 128)
+
+            def add(i, c):
+                at = pl.multiple_of(i * chunk, 8)
+                total = gw[rows_at(mine + at, chunk)]
+                for k in range(n - 1):
+                    total = total + rsb[rows_at(slot + k * part + at, chunk)]
+                gw[rows_at(mine + at, chunk)] = total
+                return c
+
+            lax.fori_loop(0, part // chunk, add, 0)
+
+        def gather_start(self, t):
+            n, idx, device_of = self.stages[t]
+            off, part, _ = self.regions[t]
+            if t == len(self.stages) - 1:
+                all_out[rows_at(self.own, self.size)] = gw[
+                    rows_at(self.own, self.size)
+                ]
+            mine = all_out.at[rows_at(off + idx * part, part)]
+            for k in range(1, n):
+                pltpu.make_async_remote_copy(
+                    mine,
+                    mine,
+                    ag_send.at[self.number, t],
+                    ag_recv.at[self.number, t],
+                    device_id=device_of(lax.rem(idx + k, n)),
+                    device_id_type=MESH,
+                ).start()
+
+        def gather_finish(self, t):
+            n, _, _ = self.stages[t]
+            _, part, slot = self.regions[t]
+            got = rsb.at[pl.ds(slot, (n - 1) * part)]
+            pltpu.make_async_copy(got, got, ag_recv.at[self.number, t]).wait()
+            pltpu.make_async_copy(got, got, ag_send.at[self.number, t]).wait()
+
+        def moves(self):
+            for t in range(len(self.stages)):
+                yield partial(self.scatter_start, t)
+                yield partial(self.scatter_finish, t)
+            for t in reversed(range(len(self.stages))):
+                yield partial(self.gather_start, t)
+                yield partial(self.gather_finish, t)
+
+    def take_steps(job, n):
+        for _ in range(n):
+            job.done += 1
+            job.todo[job.done - 1]()
+
+    def drain(jobs):
+        while any(job.done < len(job.todo) for job in jobs):
+            for job in jobs:
+                left_over = len(job.todo) - job.done
+                take_steps(job, min(left_over, 1 + (job.done % 2 and left_over > 1)))
+
+    jobs, late, middle, early = [], [], [], []
+    for k, (base, size, order, kind) in enumerate(job_plan(all_rows, unit)):
+        jobs.append(Job(k, base, size, order))
+        (late, middle, early)[kind].append(jobs[-1])
+    points = (
+        ((early, 1),),
+        ((early, 2),),
+        ((middle, 1),),
+        ((early, 2), (middle, 2)),
+        ((late, 1),),
+        ((late, 2),),
+    )
+
+    def advance(k):
+        for some, n in points[k]:
+            for job in some:
+                take_steps(job, n)
+
     at_f, at_v, at_cf, at_cv, at_m = (
         k * VARS for k in (0, 1, 3, 4, 6)
     )
@@ -744,8 +905,10 @@
             t_h[L : L + R],
             t_l[L : L + R],
         )
+        pl.when(s == 0)(lambda: advance(0))
         sums = sum_wait(s * 4 + 2)
         halo_wait(hb + 4, de1, s, 1)
+        pl.when(s == 0)(lambda: advance(1))
         grad1 = norm_rest(
             s, 1, h1[s, L : L + R1], mask[L : L + R1], de1[s, L : L + R1], sums
         )
@@ -760,14 +923,26 @@
         add_conv_grad(
             conv_base, a1h[s], a1l[s], t_h[L : L + R], t_l[L : L + R]
         )
+        pl.when(s == 0)(lambda: advance(2))
         sums = sum_wait(s * 4 + 3)
         halo_wait(hb + 5, de0, s, 2)
+
+        @pl.when(s == 0)
+        def _():
+            advance(3)
+
         grad0 = norm_rest(s, 0, h0[s], mask[...], de0[s], sums)
         bias_acc[0:1] += jnp.sum(grad0[2 * L : 2 * L + R], axis=0, keepdims=True)
         t_h, t_l = lat_triple(grad0)
         add_conv_grad(
             lift_base, xh[s], xl[s], t_h[2 * L : 2 * L + R], t_l[2 * L : 2 * L + R]
         )
+
+        @pl.when(s == 0)
+        def _():
+            gw[ch - 28 : ch - 26] = bias_acc[...]
+            advance(4)
+
         dx = conv_back(t_h, t_l, R1, w3t[0])
         lane = lane_of(R)
         own = dx[L : L + R]
@@ -812,9 +987,7 @@
 
     lax.fori_loop(0, SECTIONS, backward, 0)
 
-    gw[ch - 28 : ch - 27] = bias_acc[0:1]
-    gw[ch - 27 : ch - 26] = bias_acc[1:2]
-    weights_out = all_out.at[: gw.shape[0]]
+    advance(5)
     all_out[gw.shape[0] : gw.shape[0] + 4] = norm_acc[...].reshape(4, ch)
     lane = lane_of(R)
     new, grad = acc[...], grad_ref[...]
@@ -835,82 +1008,7 @@
             x[:at_m], jnp.zeros((at_m, ch - L), f32)
         )
 
-    stages = []
-    step = 1
-    for n in factors(nl):
-        idx = lax.rem(me_l // step, n)
-
-        def at(k, idx=idx, n=n, step=step):
-            q = lax.rem(idx + k, n)
-            return q, (me_l + (q - idx) * step, me_b)
-
-        stages.append((n, idx, at))
-        step *= n
-    step = 1
-    for n in factors(nb):
-        idx = lax.rem(me_b // step, n)
-
-        def at(k, idx=idx, n=n, step=step):
-            q = lax.rem(idx + k, n)
-            return q, (me_l, me_b + (q - idx) * step)
-
-        stages.append((n, idx, at))
-        step *= n
-    size = gw.shape[0]
-    off = 0
-    slot = 0
-    regions = []
-    for t, (n, idx, at) in enumerate(stages):
-        part = size // n
-        for k in range(1, n):
-            q, device = at(k)
-            pltpu.make_async_remote_copy(
-                gw.at[pl.ds(pl.multiple_of(off + q * part, 8), part)],
-                rsb.at[pl.ds(slot + (n - 1 - k) * part, part)],
-                rs_send.at[t],
-                rs_recv.at[t],
-                device_id=device,
-                device_id_type=MESH,
-            ).start()
-        got = rsb.at[pl.ds(slot, (n - 1) * part)]
-        pltpu.make_async_copy(got, got, rs_recv.at[t]).wait()
-        pltpu.make_async_copy(got, got, rs_send.at[t]).wait()
-        regions.append((off, size, part))
-        off = off + idx * part
-        chunk = math.gcd(part, 256)
-
-        def add(i, c, off=off, slot=slot, n=n, part=part, chunk=chunk):
-            at_row = pl.multiple_of(i * chunk, 8)
-            total = gw[pl.ds(pl.multiple_of(off + at_row, 8), chunk)]
-            for k in range(n - 1):
-                total = total + rsb[
-                    pl.ds(pl.multiple_of(slot + k * part + at_row, 8), chunk)
-                ]
-            gw[pl.ds(pl.multiple_of(off + at_row, 8), chunk)] = total
-            return c
-
-        lax.fori_loop(0, part // chunk, add, 0)
-        slot += (n - 1) * part
-        size = part
-    weights_out[pl.ds(pl.multiple_of(off, 8), size)] = gw[
-        pl.ds(pl.multiple_of(off, 8), size)
-    ]
-    for t in reversed(range(len(stages))):
-        n, idx, at = stages[t]
-        base, _, part = regions[t]
-        mine = weights_out.at[pl.ds(pl.multiple_of(base + idx * part, 8), part)]
-        for k in range(1, n):
-            pltpu.make_async_remote_copy(
-                mine,
-                mine,
-                ag_send.at[t],
-                ag_recv.at[t],
-                device_id=at(k)[1],
-                device_id_type=MESH,
-            ).start()
-        got = rsb.at[pl.ds(0, (n - 1) * part)]
-        pltpu.make_async_copy(got, got, ag_recv.at[t]).wait()
-        pltpu.make_async_copy(got, got, ag_send.at[t]).wait()
+    drain(jobs)
 
 
 def hand_out(rows, weights, *outs):
@@ -974,7 +1072,8 @@
     S = SECTIONS
     rows = 32 * ch
     rows = -(-rows // (8 * nd)) * 8 * nd
-    stage_count = len(factors(nl)) + len(factors(nb))
+    stage_count = len(factors(nl, 2)) + len(factors(nb, 4))
+    job_count = len(job_plan(rows, 8 * nd))
     vm = pltpu.VMEM
     dma = pltpu.SemaphoreType.DMA
     scratch = [
@@ -1050,10 +1149,10 @@
         dma((4 * S + 1,)),
         dma((6 * S, 2)),
         dma((6 * S, 2)),
-        dma((stage_count,)),
-        dma((stage_count,)),
-        dma((stage_count,)),
-        dma((stage_count,)),
+        dma((job_count, stage_count)),
+        dma((job_count, stage_count)),
+        dma((job_count, stage_count)),
+        dma((job_count, stage_count)),
     ]
     whole = pl.BlockSpec(memory_space=pltpu.VMEM)
     apart = pl.BlockSpec(memory_space=pl.ANY)

time: 221 us -> 173 us (0.78); the launches traced: 218 us -> 173 us
  Pallas kernels: 216 us -> 171 us
    pallas_call x1, Pallas kernels: 214 us -> 169 us  [on_device(): pl.pallas_call(partial(kernel, (nl, nb, L, W, HEADS)), out_shape=jax.Shap...]
where the time goes in v3:
time: 173 us
  Pallas kernels  171 us (99%)
    pallas_call x1, Pallas kernels, on_device(): pl.pallas_call(partial(kernel, (nl, nb, L, W, HEADS)), out_shape=jax.Shap...  169 us

profile of v3, /device:TPU:0, one launch (start us, length us, event | category | flops | bytes accessed | tf_op | source)
XLA Modules:
  0.0 173.0 jit_solution(11979924640571379953)
XLA Ops:
  0.7 169.3 %shard_map.255.weights = f32[4584,128]{1,0:T(8,128)} custom-call(f32[80,32]{1,0:T(8,128)} %bitcast.55, f32[160,32]{1,0:T(8,128)} %bitcast.52, f32[80,32]{1,0:T(8,128)} %bitcast.56, f32[160,32]{1,0:T(8,128)} %bitcast.53, s32[16,32]{1,0:T(8,128)} %bitcast.57, f32[512,75]{1,0:T(8,128)} %bitcast.51, s32[16,8,32]{2,1,0:T(8,128)} %bitcast.54, ...), custom_call_target="tpu_custom_call" | custom-call | tf_op jit(solution)/shard_map/pallas_call | solution.py:1159
  170.0 0.0 copy-start
  170.0 1.7 copy-done
  171.6 1.4 shard_map.256
Async XLA Ops:
  170.0 1.7 copy-start

commit v4 on v3

--- a/solution.py
+++ b/solution.py
@@ -124,6 +124,14 @@
     blend,
     dbh,
     dbl,
+    gh,
+    gl,
+    dh3h,
+    dh3l,
+    th,
+    tl,
+    lift_th,
+    lift_tl,
     dqkv,
     dh2,
     h2,
@@ -263,9 +271,19 @@
     def lroll(x, shift):
         return pltpu.roll(x, shift % LANES, 1)
 
-    def conv(hi, lo, base, n, weights):
-        cols_h = [hi[base + j * L : base + j * L + n] for j in range(3)]
-        cols_l = [lo[base + j * L : base + j * L + n] for j in range(3)]
+    def rows_of(ref, ranges, base=0):
+        parts = [ref[base + a : base + b] for a, b in ranges]
+        return parts[0] if len(parts) == 1 else jnp.concatenate(parts, axis=0)
+
+    def put_rows(ref, value, ranges, base=0):
+        at = 0
+        for a, b in ranges:
+            ref[base + a : base + b] = value[at : at + b - a]
+            at += b - a
+
+    def conv(hi, lo, ranges, weights):
+        cols_h = [rows_of(hi, ranges, j * L) for j in range(3)]
+        cols_l = [rows_of(lo, ranges, j * L) for j in range(3)]
         wide = dot(lanes_cat(*cols_h, *cols_l, *cols_h), weights)
         return (
             wide[:, ch : 2 * ch]
@@ -273,9 +291,10 @@
             + north(wide[:, 2 * ch :])
         )
 
-    def product(x, weights):
-        hi, lo = split(x)
-        return dot(lanes_cat(hi, lo, hi), weights)
+    def product(hi, lo, weights):
+        wide = dot(lanes_cat(hi, lo), weights)
+        n = wide.shape[1] // 2
+        return wide[:, :n] + wide[:, n:]
 
     def rows_product(ah, al, gh, gl):
         t = ((0,), (0,))
@@ -284,13 +303,20 @@
     def lat_triple(x):
         return split(lanes_cat(north(x), x, south(x)))
 
-    def conv_back(gh, gl, n, weights):
+    def conv_back(hi, lo, ranges, weights):
+        wider = [(a, b + 2 * L) for a, b in ranges]
+        gh, gl = rows_of(hi, wider), rows_of(lo, wider)
         wide = dot(lanes_cat(gh, gl, gh), weights)
-        return (
-            wide[2 * L : 2 * L + n, :ch]
-            + wide[L : L + n, ch : 2 * ch]
-            + wide[:n, 2 * ch :]
-        )
+        outs, at = [], 0
+        for a, b in ranges:
+            n = b - a
+            outs.append(
+                wide[at + 2 * L : at + 2 * L + n, :ch]
+                + wide[at + L : at + L + n, ch : 2 * ch]
+                + wide[at : at + n, 2 * ch :]
+            )
+            at += n + 2 * L
+        return outs
 
     def add_conv_grad(base, ah, al, gh, gl):
         for j in range(3):
@@ -519,23 +545,29 @@
     halo_start(0, ys, 0, 2)
     sum_start(4 * SECTIONS, jnp.concatenate([count_part, count_part], axis=0))
 
-    def put_three(target, w):
-        n = w.shape[0]
+    def square(hi, lo):
+        return jnp.concatenate(
+            [lanes_cat(hi, lo), lanes_cat(hi, jnp.zeros_like(hi))], axis=0
+        )
+
+    def put_square(target, w):
+        n, m = w.shape
         hi, lo = split(w)
-        target[:n] = hi
-        target[n : 2 * n] = hi
-        target[2 * n :] = lo
+        target[:n, :m] = hi
+        target[:n, m:] = lo
+        target[n:, :m] = hi
+        target[n:, m:] = jnp.zeros_like(hi)
 
     for load in loads[8:]:
         load.wait()
-    put_three(wq3, qkv_ref[...])
-    put_three(wqt3, qkv_ref[...].T)
-    put_three(wo3, out_ref[...])
-    put_three(wot3, out_ref[...].T)
+    put_square(wq3, qkv_ref[...])
+    put_square(wqt3, qkv_ref[...].T)
+    put_square(wo3, out_ref[...])
+    put_square(wot3, out_ref[...].T)
     tap[...] = jnp.zeros_like(tap)
     tap[3 * VARS : 5 * VARS] = head_ref[...]
-    put_three(wht3, tap[...])
-    put_three(wh3, tap[...].T)
+    put_square(wht3, tap[...])
+    put_square(wh3, tap[...].T)
     head_bias_row[...] = jnp.zeros_like(head_bias_row)
     head_bias_row[:, 3 * VARS : 5 * VARS] = head_bias_ref[...]
     for s, weight in enumerate((1.0, 2.0, 2.0, 1.0)):
@@ -577,8 +609,8 @@
     gains = [gain_ref[0:1], gain_ref[1:2]]
     shifts = [shift_ref[0:1], shift_ref[1:2]]
 
-    def stats(h):
-        weighted = h * mask[2 * L : 2 * L + R]
+    def stats(h, ranges):
+        weighted = h * rows_of(mask, ranges, 2 * L)
         return jnp.concatenate(
             [
                 jnp.sum(weighted, axis=0, keepdims=True),
@@ -604,34 +636,48 @@
         )
         return z * below, slope
 
-    group = 2
+    last = W // 2 - 1
+    all_own = [(0, R)]
+    own_edges, own_inner = [(0, pair), (R - pair, R)], [(pair, R - pair)]
 
     def forward(s, carry):
         hb = s * 6
-
-        halo_wait(hb, ys, s, 2)
+        ext = 2 * pair
+
+        def lift(ranges):
+            value = conv(xh.at[s], xl.at[s], ranges, w3f[0]) + lift_bias
+            put_rows(h0.at[s], value, ranges, 2 * L)
+            return stats(value, ranges)
+
+        def lay(a, b):
+            y = ys[s, L + a : L + b]
+            lane = lane_of(b - a)
+            lon = 0.5 * (ys[s, 2 * L + a : 2 * L + b] - ys[s, a:b])
+            x = jnp.where(
+                (lane >= VARS) & (lane < 2 * VARS),
+                lat_diff(y),
+                jnp.where((lane >= 2 * VARS) & (lane < 3 * VARS), lon, y),
+            )
+            hi, lo = split(x)
+            xh[s, a:b] = hi
+            xl[s, a:b] = lo
 
         @pl.when(s == 0)
         def _():
+            halo_wait(hb, ys, s, 2)
             mask[...] = jnp.broadcast_to(
                 ys[0, :, MASK_LANE : MASK_LANE + 1], (R2, LANES)
             )
 
+        lay(pair, R1 - pair)
+        sums = lift(own_inner)
+        pl.when(s > 0)(lambda: halo_wait(hb, ys, s, 2))
+        lay(0, pair)
+        lay(R1 - pair, R1)
+        sum_start(s * 4, sums + lift(own_edges))
+        halo_start(hb + 1, h0, s, 2)
         y1 = ys[s, L : L + R1]
         lane = lane_of(R1)
-        lon = 0.5 * (ys[s, 2 * L : 2 * L + R1] - ys[s, 0:R1])
-        x = jnp.where(
-            (lane >= VARS) & (lane < 2 * VARS),
-            lat_diff(y1),
-            jnp.where((lane >= 2 * VARS) & (lane < 3 * VARS), lon, y1),
-        )
-        hi, lo = split(x)
-        xh[s] = hi
-        xl[s] = lo
-        first = conv(xh.at[s], xl.at[s], 0, R, w3f[0]) + lift_bias
-        h0[s, 2 * L : 2 * L + R] = first
-        sum_start(s * 4, stats(first))
-        halo_start(hb + 1, h0, s, 2)
         flux = y1 * lroll(y1, -3 * VARS)
         flux = jnp.where(lane < 2 * VARS, flux, 0.0)
         own_lane = lane_of(R)
@@ -641,7 +687,6 @@
         )
         t = -(t_lat + lroll(t_lon, -VARS))
         tend[...] = t + lroll(t, VARS) + lroll(t, 2 * VARS)
-
 
         @pl.when(s == 0)
         def _():
@@ -654,9 +699,11 @@
         hi, lo = split(act)
         a1h[s] = hi
         a1l[s] = lo
-        second = h0[s, 2 * L : 2 * L + R] + conv(a1h.at[s], a1l.at[s], 0, R, w3f[1])
+        second = h0[s, 2 * L : 2 * L + R] + conv(
+            a1h.at[s], a1l.at[s], all_own, w3f[1]
+        )
         h1[s, 2 * L : 2 * L + R] = second
-        sum_start(s * 4 + 1, stats(second))
+        sum_start(s * 4 + 1, stats(second, all_own))
         halo_start(hb + 2, h1, s, 2)
         average, inverse = normalise(s, 1, sum_wait(s * 4 + 1))
         halo_wait(hb + 2, h1, s, 2)
@@ -665,30 +712,34 @@
         hi, lo = split(act)
         a2h[s] = hi
         a2l[s] = lo
-        third = h1[s, L : L + R1] + conv(a2h.at[s], a2l.at[s], 0, R1, w3f[2])
-        h2[...] = third
-        hi, lo = split(third)
-        h2h[s] = hi
-        h2l[s] = lo
-        mixing = dot(lanes_cat(hi, lo, hi), wq3[...])
-        hi, lo = split(mixing[L : L + R, :ch] * scale)
-        qh[s] = hi
-        ql[s] = lo
-        hi, lo = split(mixing[:, ch : 2 * ch])
-        kh[s] = hi
-        kl[s] = lo
-        hi, lo = split(mixing[:, 2 * ch :])
-        vh[s] = hi
-        vl[s] = lo
+
+        def second_block(ranges):
+            third = rows_of(h1.at[s], ranges, L) + conv(
+                a2h.at[s], a2l.at[s], ranges, w3f[2]
+            )
+            put_rows(h2, third, ranges)
+            hi, lo = split(third)
+            put_rows(h2h.at[s], hi, ranges)
+            put_rows(h2l.at[s], lo, ranges)
+            mixing = product(hi, lo, wq3[...])
+            hi, lo = split(mixing[:, :ch] * scale)
+            put_rows(qh.at[s], hi, ranges)
+            put_rows(ql.at[s], lo, ranges)
+            hi, lo = split(mixing[:, ch : 2 * ch])
+            put_rows(kh.at[s], hi, ranges)
+            put_rows(kl.at[s], lo, ranges)
+            hi, lo = split(mixing[:, 2 * ch :])
+            put_rows(vh.at[s], hi, ranges)
+            put_rows(vl.at[s], lo, ranges)
 
         def attend(pairs):
             scores = []
             for p in pairs:
-                at = pl.multiple_of(p * pair, pair)
-                q_h = per_head(qh[s, pl.ds(at, pair)])
-                q_l = per_head(ql[s, pl.ds(at, pair)])
-                k_h = kh[s, pl.ds(at, 2 * pair)]
-                k_l = kl[s, pl.ds(at, 2 * pair)]
+                at = p * pair
+                q_h = per_head(qh[s, at + L : at + L + pair])
+                q_l = per_head(ql[s, at + L : at + L + pair])
+                k_h = kh[s, at : at + ext]
+                k_l = kl[s, at : at + ext]
                 scores.append(
                     dot(
                         lanes_cat(k_h, k_l, k_h),
@@ -704,65 +755,48 @@
                 probs[s, p] = e
                 weights.append(e)
             for p, e in zip(pairs, weights):
-                at = pl.multiple_of(p * pair, pair)
+                at = p * pair
                 p_h, p_l = split(e.T)
-                v_h = vh[s, pl.ds(at, 2 * pair)]
-                v_l = vl[s, pl.ds(at, 2 * pair)]
-                o = dot(
-                    lanes_cat(p_h, p_l, p_h),
-                    jnp.concatenate([v_h, v_h, v_l], axis=0),
-                )
-                blend[pl.ds(at, pair)] = heads_sum(o)
+                v_h = vh[s, at : at + ext]
+                v_l = vl[s, at : at + ext]
+                o = product(p_h, p_l, square(v_h, v_l))
+                blend[at : at + pair] = heads_sum(o)
 
         weight = jnp.where((s == 0) | (s == SECTIONS - 1), 1.0, 2.0)
         factor = jnp.where(s == SECTIONS - 2, 1.0, 0.5) * step_size
 
         def finish(ranges):
-            def take(ref, base=0):
-                return jnp.concatenate(
-                    [ref[base + a : base + b] for a, b in ranges], axis=0
-                )
-
-            def give(ref, value, base=0):
-                at = 0
-                for a, b in ranges:
-                    ref[base + a : base + b] = value[at : at + b - a]
-                    at += b - a
-
-            hi, lo = split(take(blend))
-            give(bh.at[s], hi)
-            give(bl.at[s], lo)
-            fourth = take(h2, L) + dot(lanes_cat(hi, lo, hi), wo3[...])
+            hi, lo = split(rows_of(blend, ranges))
+            put_rows(bh.at[s], hi, ranges)
+            put_rows(bl.at[s], lo, ranges)
+            fourth = rows_of(h2, ranges, L) + product(hi, lo, wo3[...])
             hi, lo = split(fourth)
-            give(h3h.at[s], hi)
-            give(h3l.at[s], lo)
+            put_rows(h3h.at[s], hi, ranges)
+            put_rows(h3l.at[s], lo, ranges)
             slope_now = (
-                take(tend) + dot(lanes_cat(hi, lo, hi), wh3[...]) + head_bias
+                rows_of(tend, ranges)
+                + product(hi, lo, wh3[...])
+                + head_bias
             )
-            give(acc, take(acc) + weight * slope_now)
-
-            @pl.when(s < SECTIONS - 1)
-            def _():
-                give(
-                    ys.at[s + 1],
-                    take(ys.at[0], 2 * L) + factor * slope_now,
-                    2 * L,
-                )
-
-        last = W // 2 - 1
+            put_rows(acc, rows_of(acc, ranges) + weight * slope_now, ranges)
+            put_rows(
+                ys.at[s + 1],
+                rows_of(ys.at[0], ranges, 2 * L) + factor * slope_now,
+                ranges,
+                2 * L,
+            )
+
+        second_block([(0, ext), (R1 - ext, R1)])
         attend([0, last])
-        finish([(0, pair), (R - pair, R)])
+        finish(own_edges)
 
         @pl.when(s < SECTIONS - 1)
         def _():
             halo_start(hb + 6, ys, s + 1, 2)
 
-        def inner(k, c):
-            attend([1 + group * k + m for m in range(group)])
-            return c
-
-        lax.fori_loop(0, (last - 1) // group, inner, 0)
-        finish([(pair, R - pair)])
+        second_block([(ext, R1 - ext)])
+        attend(range(1, last))
+        finish(own_inner)
         return carry
 
     lax.fori_loop(0, SECTIONS, forward, 0)
@@ -794,19 +828,26 @@
     def backward(turn, carry):
         s = SECTIONS - 1 - turn
         hb = s * 6
-        g = gk[s]
-        g_h, g_l = split(g)
-        grad3 = dot(lanes_cat(g_h, g_l, g_h), wht3[...])
-        grad3_h, grad3_l = split(grad3)
-        hi, lo = split(dot(lanes_cat(grad3_h, grad3_l, grad3_h), wot3[...]))
-        dbh[...] = hi
-        dbl[...] = lo
+        g_h, g_l = split(gk[s])
+        gh[...] = g_h
+        gl[...] = g_l
         dqkv[...] = jnp.zeros_like(dqkv)
+
+        def head_back(ranges):
+            hi, lo = rows_of(gh, ranges), rows_of(gl, ranges)
+            grad3 = product(hi, lo, wht3[...])
+            hi, lo = split(grad3)
+            put_rows(dh2, grad3, ranges, L)
+            put_rows(dh3h, hi, ranges)
+            put_rows(dh3l, lo, ranges)
+            hi, lo = split(product(hi, lo, wot3[...]))
+            put_rows(dbh, hi, ranges)
+            put_rows(dbl, lo, ranges)
 
         def attend_back(pairs):
             dps = []
             for p in pairs:
-                at = pl.multiple_of(p * pair, pair)
+                at = p * pair
                 d_h = per_head(dbh[pl.ds(at, pair)])
                 d_l = per_head(dbl[pl.ds(at, pair)])
                 v_h = vh[s, pl.ds(at, 2 * pair)]
@@ -823,17 +864,14 @@
                 e = probs[s, p]
                 dss.append(e * (dp - jnp.sum(e * dp, axis=0, keepdims=True)))
             for p, ds in zip(pairs, dss):
-                at = pl.multiple_of(p * pair, pair)
+                at = p * pair
                 k_h = kh[s, pl.ds(at, 2 * pair)]
                 k_l = kl[s, pl.ds(at, 2 * pair)]
                 t_h, t_l = split(ds.T)
-                o = dot(
-                    lanes_cat(t_h, t_l, t_h),
-                    jnp.concatenate([k_h, k_h, k_l], axis=0),
-                )
+                o = product(t_h, t_l, square(k_h, k_l))
                 dqkv[pl.ds(at + L, pair), :ch] = heads_sum(o) * scale
-                q_h = per_head(qh[s, pl.ds(at, pair)])
-                q_l = per_head(ql[s, pl.ds(at, pair)])
+                q_h = per_head(qh[s, at + L : at + L + pair])
+                q_l = per_head(ql[s, at + L : at + L + pair])
                 s_h, s_l = split(ds)
                 o = dot(s_h, lanes_cat(q_h, q_l))
                 o = o[:, :ch] + o[:, ch:] + dot(s_l, q_h)
@@ -845,21 +883,25 @@
                 o = o[:, :ch] + o[:, ch:] + dot(s_l, d_h)
                 dqkv[pl.ds(at, 2 * pair), 2 * ch :] += o
 
-        last = W // 2 - 1
+        def to_hidden(ranges):
+            hi, lo = split(rows_of(dqkv, ranges))
+            part = product(hi, lo, wqt3[...])
+            put_rows(dh2, rows_of(dh2, ranges) + part, ranges)
+
+        def triple(ranges):
+            hi, lo = lat_triple(rows_of(dh2, ranges))
+            put_rows(th, hi, ranges)
+            put_rows(tl, lo, ranges)
+
+        dh2[:L] = jnp.zeros((L, ch), f32)
+        dh2[R1 - L :] = jnp.zeros((L, ch), f32)
+        head_back(own_edges)
         attend_back([0, last])
-        edge_h, edge_l = split(
-            jnp.concatenate([dqkv[:pair], dqkv[R1 - pair :]], axis=0)
-        )
-        part = dot(lanes_cat(edge_h, edge_l, edge_h), wqt3[...])
-        zeros = jnp.zeros((L, ch), f32)
-        part = part + jnp.concatenate(
-            [zeros, grad3[:L], grad3[R - L :], zeros], axis=0
-        )
-        dh2[:pair] = part[:pair]
-        dh2[R1 - pair :] = part[pair:]
-        sb[s, 0, :pair] = part[:pair]
+        border = [(0, pair), (R1 - pair, R1)]
+        to_hidden(border)
+        for side, (a, b) in enumerate(border):
+            sb[s, side, :pair] = dh2[a:b]
         sb[s, 0, pair:] = gk[s, :L]
-        sb[s, 1, :pair] = part[pair:]
         sb[s, 1, pair:] = gk[s, R - L :]
         edges = [
             side_copy(hb + 3, side, sb.at[s, side], rb.at[s, side])
@@ -867,33 +909,33 @@
         ]
         for e in edges:
             e.start()
-
-        def inner(k, c):
-            attend_back([1 + group * k + m for m in range(group)])
-            return c
-
-        lax.fori_loop(0, (last - 1) // group, inner, 0)
-        d_h, d_l = split(dqkv[...])
-        mid_h, mid_l = d_h[pair : R1 - pair], d_l[pair : R1 - pair]
-        dh2[pair : R1 - pair] = grad3[L : R - L] + dot(
-            lanes_cat(mid_h, mid_l, mid_h), wqt3[...]
+        head_back(own_inner)
+        attend_back(range(1, last))
+        to_hidden([(pair, R1 - pair)])
+        triple([(pair, R1 - pair)])
+        (inner_act,) = conv_back(th, tl, own_inner, w3t[2])
+        bias_acc[1:2] += jnp.sum(gk[s], axis=0, keepdims=True)
+        gw[head_base : head_base + ch] += rows_product(
+            h3h[s], h3l[s], gh[...], gl[...]
         )
         for e in edges:
             e.wait()
         dh2[:pair] += rb[s, 1, :pair]
         dh2[R1 - pair :] += rb[s, 0, :pair]
-
-        t_h, t_l = lat_triple(dh2[...])
-        grad_act = conv_back(t_h, t_l, R, w3t[2])
+        triple(border)
+        low_act, high_act = conv_back(th, tl, own_edges, w3t[2])
+
+        grad_act = jnp.concatenate([low_act, inner_act, high_act], axis=0)
         sums, direct = norm_back(
             s, 1, h1[s, 2 * L : 2 * L + R], grad_act, dg2[s], dh2[L : L + R]
         )
         sum_start(s * 4 + 2, sums)
         de1[s, 2 * L : 2 * L + R] = direct
         halo_start(hb + 4, de1, s, 1)
-        bias_acc[1:2] += jnp.sum(g, axis=0, keepdims=True)
-        gw[head_base : head_base + ch] += rows_product(h3h[s], h3l[s], g_h, g_l)
-        gw[out_base : out_base + ch] += rows_product(bh[s], bl[s], grad3_h, grad3_l)
+        gw[out_base : out_base + ch] += rows_product(
+            bh[s], bl[s], dh3h[...], dh3l[...]
+        )
+        d_h, d_l = split(dqkv[...])
         wide = rows_product(h2h[s], h2l[s], d_h, d_l)
         for k in range(3):
             at = qkv_base + k * ch
@@ -902,8 +944,8 @@
             conv_base + 9 * ch,
             a2h[s, L : L + R1],
             a2l[s, L : L + R1],
-            t_h[L : L + R],
-            t_l[L : L + R],
+            th[L : L + R],
+            tl[L : L + R],
         )
         pl.when(s == 0)(lambda: advance(0))
         sums = sum_wait(s * 4 + 2)
@@ -913,7 +955,7 @@
             s, 1, h1[s, L : L + R1], mask[L : L + R1], de1[s, L : L + R1], sums
         )
         t_h, t_l = lat_triple(grad1)
-        grad_act = conv_back(t_h, t_l, R, w3t[1])
+        (grad_act,) = conv_back(t_h, t_l, all_own, w3t[1])
         sums, direct = norm_back(
             s, 0, h0[s, 2 * L : 2 * L + R], grad_act, dg1[s], grad1[L : L + R]
         )
@@ -923,6 +965,11 @@
         add_conv_grad(
             conv_base, a1h[s], a1l[s], t_h[L : L + R], t_l[L : L + R]
         )
+
+        def lift_grad(s):
+            add_conv_grad(lift_base, xh[s], xl[s], lift_th[...], lift_tl[...])
+
+        pl.when(s < SECTIONS - 1)(lambda: lift_grad(s + 1))
         pl.when(s == 0)(lambda: advance(2))
         sums = sum_wait(s * 4 + 3)
         halo_wait(hb + 5, de0, s, 2)
@@ -934,16 +981,16 @@
         grad0 = norm_rest(s, 0, h0[s], mask[...], de0[s], sums)
         bias_acc[0:1] += jnp.sum(grad0[2 * L : 2 * L + R], axis=0, keepdims=True)
         t_h, t_l = lat_triple(grad0)
-        add_conv_grad(
-            lift_base, xh[s], xl[s], t_h[2 * L : 2 * L + R], t_l[2 * L : 2 * L + R]
-        )
+        lift_th[...] = t_h[2 * L : 2 * L + R]
+        lift_tl[...] = t_l[2 * L : 2 * L + R]
 
         @pl.when(s == 0)
         def _():
+            lift_grad(s)
             gw[ch - 28 : ch - 26] = bias_acc[...]
             advance(4)
 
-        dx = conv_back(t_h, t_l, R1, w3t[0])
+        (dx,) = conv_back(t_h, t_l, [(0, R1)], w3t[0])
         lane = lane_of(R)
         own = dx[L : L + R]
         lon = 0.5 * (dx[2 * L :] - dx[:R])
@@ -1077,7 +1124,7 @@
     vm = pltpu.VMEM
     dma = pltpu.SemaphoreType.DMA
     scratch = [
-        vm((S, R2, ch), f32),
+        vm((S + 1, R2, ch), f32),
         vm((S, R1, ch), bf16),
         vm((S, R1, ch), bf16),
         vm((S, R2, ch), f32),
@@ -1090,8 +1137,8 @@
         vm((S, R, ch), f32),
         vm((S, R1, ch), bf16),
         vm((S, R1, ch), bf16),
-        vm((S, R, ch), bf16),
-        vm((S, R, ch), bf16),
+        vm((S, R1, ch), bf16),
+        vm((S, R1, ch), bf16),
         vm((S, R1, ch), bf16),
         vm((S, R1, ch), bf16),
         vm((S, R1, ch), bf16),
@@ -1109,16 +1156,24 @@
         vm((W // 2, 4 * L, 2 * HEADS * L), f32),
         vm((3, 9 * ch, 3 * ch), bf16),
         vm((3, 9 * ch, 3 * ch), bf16),
-        vm((3 * ch, 3 * ch), bf16),
-        vm((9 * ch, ch), bf16),
-        vm((3 * ch, ch), bf16),
-        vm((3 * ch, ch), bf16),
-        vm((3 * ch, ch), bf16),
-        vm((3 * ch, ch), bf16),
+        vm((2 * ch, 6 * ch), bf16),
+        vm((6 * ch, 2 * ch), bf16),
+        vm((2 * ch, 2 * ch), bf16),
+        vm((2 * ch, 2 * ch), bf16),
+        vm((2 * ch, 2 * ch), bf16),
+        vm((2 * ch, 2 * ch), bf16),
         vm((ch, ch), f32),
         vm((R, ch), f32),
         vm((R, ch), bf16),
         vm((R, ch), bf16),
+        vm((R, ch), bf16),
+        vm((R, ch), bf16),
+        vm((R, ch), bf16),
+        vm((R, ch), bf16),
+        vm((R1, 3 * ch), bf16),
+        vm((R1, 3 * ch), bf16),
+        vm((R, 3 * ch), bf16),
+        vm((R, 3 * ch), bf16),
         vm((R1, 3 * ch), f32),
         vm((R1, ch), f32),
         vm((R1, ch), f32),

time: 173 us -> 165 us (0.954)
  Pallas kernels: 171 us -> 163 us
    pallas_call x1, Pallas kernels: 169 us -> 161 us  [on_device(): pl.pallas_call(partial(kernel, (nl, nb, L, W, HEADS)), out_shape=jax.Shap...]
where the time goes in v4:
time: 165 us
  Pallas kernels  163 us (99%)
  local copies, waits for them, and re-layouts  1.66 us (1%)
    pallas_call x1, Pallas kernels, on_device(): pl.pallas_call(partial(kernel, (nl, nb, L, W, HEADS)), out_shape=jax.Shap...  161 us

profile of v4, /device:TPU:0, one launch (start us, length us, event | category | flops | bytes accessed | tf_op | source)
XLA Modules:
  0.0 165.0 jit_solution(5272791550087649276)
XLA Ops:
  0.7 161.3 %shard_map.255.weights = f32[4584,128]{1,0:T(8,128)} custom-call(f32[80,32]{1,0:T(8,128)} %bitcast.55, f32[160,32]{1,0:T(8,128)} %bitcast.52, f32[80,32]{1,0:T(8,128)} %bitcast.56, f32[160,32]{1,0:T(8,128)} %bitcast.53, s32[16,32]{1,0:T(8,128)} %bitcast.57, f32[512,75]{1,0:T(8,128)} %bitcast.51, s32[16,8,32]{2,1,0:T(8,128)} %bitcast.54, ...), custom_call_target="tpu_custom_call" | custom-call | tf_op jit(solution)/shard_map/pallas_call | solution.py:1214
  161.9 0.0 copy-start
  162.0 1.7 %copy-done = f32[4584,128]{1,0:T(8,128)S(1)} copy-done((f32[4584,128]{1,0:T(8,128)S(1)}, f32[4584,128]{1,0:T(8,128)}, u32[]{:S(2)}) %copy-start) | copy-done | bytes 2347032
  163.6 1.4 shard_map.256
Async XLA Ops:
  161.9 1.7 %copy-start = (f32[4584,128]{1,0:T(8,128)S(1)}, f32[4584,128]{1,0:T(8,128)}, u32[]{:S(2)}) copy-start(f32[4584,128]{1,0:T(8,128)} %shard_map.255.weights) | copy-start | bytes 7041028

commit v5 on v4

--- a/solution.py
+++ b/solution.py
@@ -13,6 +13,8 @@
 LANES = 128
 VARS = 5
 MASK_LANE = 127
+HEAD_ROWS = 32
+LIFT_BACK = 32
 epsilon = 1e-05
 step_size = 0.25
 f32 = jnp.float32
@@ -43,18 +45,26 @@
     return out
 
 
-def job_plan(rows, unit):
-    late = -(-9 * LANES // unit)
-    middle = -(-18 * LANES // unit) - late
+def tap_rows(cin):
+    return -(-(cin + 2) // 8) * 8
+
+
+def bases(cin):
+    conv = 9 * tap_rows(cin)
+    qkv = conv + 18 * LANES
+    out = qkv + 3 * LANES
+    return conv, qkv, out, out + LANES
+
+
+def job_plan(rows, unit, cin):
+    conv = bases(cin)[0]
+    late = -(-conv // unit)
+    middle = -(-(conv + 9 * LANES) // unit) - late
     early = rows // unit - late - middle
-    split_late, split_early = (late + 1) // 2, (early + 1) // 2
-    sizes = (
-        (split_late, "A", 0),
-        (late - split_late, "B", 0),
-        (middle, "C", 1),
-        (split_early, "A", 2),
-        (early - split_early, "B", 2),
-    )
+    sizes = []
+    for kind, units in enumerate((late, middle, early)):
+        half = (units + 1) // 2
+        sizes += [(half, "A", kind), (units - half, "B", kind)]
     plan, at = [], 0
     for units, order, kind in sizes:
         if units:
@@ -81,7 +91,7 @@
     head_bias_ref,
     gain_ref,
     shift_ref,
-    all_out,
+    final_out,
     ys,
     xh,
     xl,
@@ -114,6 +124,7 @@
     mult,
     w3f,
     w3t,
+    lift_t,
     wq3,
     wqt3,
     wo3,
@@ -144,6 +155,8 @@
     rsb,
     norm_acc,
     bias_acc,
+    all_out,
+    out_sems,
     planes,
     mask_plane,
     context_ref,
@@ -318,18 +331,17 @@
             at += n + 2 * L
         return outs
 
-    def add_conv_grad(base, ah, al, gh, gl):
+    def add_conv_grad(base, ah, al, gh, gl, taken=ch):
         for j in range(3):
             part = rows_product(
                 ah[j * L : j * L + R], al[j * L : j * L + R], gh, gl
             )
             for i in range(3):
-                at = base + (i * 3 + j) * ch
-                gw[at : at + ch, :] += part[:, i * ch : (i + 1) * ch]
-
-    lift_base, conv_base = 0, 9 * ch
-    qkv_base = 27 * ch
-    out_base, head_base = 30 * ch, 31 * ch
+                at = base + (i * 3 + j) * taken
+                gw[at : at + taken, :] += part[:taken, i * ch : (i + 1) * ch]
+
+    cin = lift_in.shape[2]
+    conv_base, qkv_base, out_base, head_base = bases(cin)
 
     all_rows = gw.shape[0]
     unit = 8 * nd
@@ -356,7 +368,6 @@
     orders = {
         "A": first + rest,
         "B": first + rest[1::-1] + rest[2:],
-        "C": first + rest[::-1],
     }
 
     def rows_at(at, n):
@@ -365,6 +376,11 @@
     class Job:
         def __init__(self, number, base, size, order):
             self.number = number
+            self.result = pltpu.make_async_copy(
+                all_out.at[base : base + size],
+                final_out.at[base : base + size],
+                out_sems.at[number],
+            )
             self.stages = stages = [stage_of(m) for m in orders[order]]
             self.regions = []
             off, slot = base, base
@@ -435,13 +451,17 @@
             pltpu.make_async_copy(got, got, ag_recv.at[self.number, t]).wait()
             pltpu.make_async_copy(got, got, ag_send.at[self.number, t]).wait()
 
+        def finished(self):
+            self.gather_finish(0)
+            self.result.start()
+
         def moves(self):
             for t in range(len(self.stages)):
                 yield partial(self.scatter_start, t)
                 yield partial(self.scatter_finish, t)
             for t in reversed(range(len(self.stages))):
                 yield partial(self.gather_start, t)
-                yield partial(self.gather_finish, t)
+                yield partial(self.gather_finish, t) if t else self.finished
 
     def take_steps(job, n):
         for _ in range(n):
@@ -455,7 +475,7 @@
                 take_steps(job, min(left_over, 1 + (job.done % 2 and left_over > 1)))
 
     jobs, late, middle, early = [], [], [], []
-    for k, (base, size, order, kind) in enumerate(job_plan(all_rows, unit)):
+    for k, (base, size, order, kind) in enumerate(job_plan(all_rows, unit, lift_in.shape[2])):
         jobs.append(Job(k, base, size, order))
         (late, middle, early)[kind].append(jobs[-1])
     points = (
@@ -519,11 +539,13 @@
     mask_own = jnp.broadcast_to(
         ys[0, 2 * L : 2 * L + R, MASK_LANE : MASK_LANE + 1], (R, LANES)
     )
+    mask[2 * L : 2 * L + R] = mask_own
     count_part = jnp.sum(mask_own, axis=0, keepdims=True)
     for load in loads[6:8]:
         load.wait()
 
     tap[...] = jnp.zeros_like(tap)
+    lift_t[...] = jnp.zeros_like(lift_t)
     for b in range(3):
         for i in range(3):
             for j in range(3):
@@ -537,9 +559,18 @@
                     at = (p * 3 + j) * ch
                     w3f[b, at : at + ch, i * ch : (i + 1) * ch] = part
                 hi, lo = split(w.T)
+                if b == 0:
+                    cols = slice(j * LIFT_BACK, (j + 1) * LIFT_BACK)
+                    hi, lo = hi[:, :LIFT_BACK], lo[:, :LIFT_BACK]
+                    at, below = i * ch, (3 + i) * ch
+                    lift_t[at : at + ch, cols] = hi
+                    lift_t[below : below + ch, cols] = hi
+                    cols = slice(ch + cols.start, ch + cols.stop)
+                    lift_t[at : at + ch, cols] = lo
+                    continue
                 for p, part in enumerate((hi, hi, lo)):
                     at = (p * 3 + i) * ch
-                    w3t[b, at : at + ch, j * ch : (j + 1) * ch] = part
+                    w3t[b - 1, at : at + ch, j * ch : (j + 1) * ch] = part
 
     pl.semaphore_wait(barrier, nd - 1)
     halo_start(0, ys, 0, 2)
@@ -662,16 +693,9 @@
             xh[s, a:b] = hi
             xl[s, a:b] = lo
 
-        @pl.when(s == 0)
-        def _():
-            halo_wait(hb, ys, s, 2)
-            mask[...] = jnp.broadcast_to(
-                ys[0, :, MASK_LANE : MASK_LANE + 1], (R2, LANES)
-            )
-
         lay(pair, R1 - pair)
         sums = lift(own_inner)
-        pl.when(s > 0)(lambda: halo_wait(hb, ys, s, 2))
+        halo_wait(hb, ys, s, 2)
         lay(0, pair)
         lay(R1 - pair, R1)
         sum_start(s * 4, sums + lift(own_edges))
@@ -691,6 +715,10 @@
         @pl.when(s == 0)
         def _():
             count[...] = sum_wait(4 * SECTIONS)
+            for at in (0, R + pair):
+                mask[at : at + pair] = jnp.broadcast_to(
+                    ys[0, at : at + pair, MASK_LANE : MASK_LANE + 1], (pair, LANES)
+                )
 
         average, inverse = normalise(s, 0, sum_wait(s * 4))
         halo_wait(hb + 1, h0, s, 2)
@@ -913,17 +941,16 @@
         attend_back(range(1, last))
         to_hidden([(pair, R1 - pair)])
         triple([(pair, R1 - pair)])
-        (inner_act,) = conv_back(th, tl, own_inner, w3t[2])
+        (inner_act,) = conv_back(th, tl, own_inner, w3t[1])
         bias_acc[1:2] += jnp.sum(gk[s], axis=0, keepdims=True)
-        gw[head_base : head_base + ch] += rows_product(
-            h3h[s], h3l[s], gh[...], gl[...]
-        )
+        part = rows_product(gh[...], gl[...], h3h[s], h3l[s])
+        gw[head_base : head_base + HEAD_ROWS] += part[:HEAD_ROWS]
         for e in edges:
             e.wait()
         dh2[:pair] += rb[s, 1, :pair]
         dh2[R1 - pair :] += rb[s, 0, :pair]
         triple(border)
-        low_act, high_act = conv_back(th, tl, own_edges, w3t[2])
+        low_act, high_act = conv_back(th, tl, own_edges, w3t[1])
 
         grad_act = jnp.concatenate([low_act, inner_act, high_act], axis=0)
         sums, direct = norm_back(
@@ -955,7 +982,7 @@
             s, 1, h1[s, L : L + R1], mask[L : L + R1], de1[s, L : L + R1], sums
         )
         t_h, t_l = lat_triple(grad1)
-        (grad_act,) = conv_back(t_h, t_l, all_own, w3t[1])
+        (grad_act,) = conv_back(t_h, t_l, all_own, w3t[0])
         sums, direct = norm_back(
             s, 0, h0[s, 2 * L : 2 * L + R], grad_act, dg1[s], grad1[L : L + R]
         )
@@ -967,7 +994,9 @@
         )
 
         def lift_grad(s):
-            add_conv_grad(lift_base, xh[s], xl[s], lift_th[...], lift_tl[...])
+            add_conv_grad(
+                0, xh[s], xl[s], lift_th[...], lift_tl[...], tap_rows(cin)
+            )
 
         pl.when(s < SECTIONS - 1)(lambda: lift_grad(s + 1))
         pl.when(s == 0)(lambda: advance(2))
@@ -987,10 +1016,15 @@
         @pl.when(s == 0)
         def _():
             lift_grad(s)
-            gw[ch - 28 : ch - 26] = bias_acc[...]
+            gw[cin : cin + 2] = bias_acc[...]
             advance(4)
 
-        (dx,) = conv_back(t_h, t_l, [(0, R1)], w3t[0])
+        wide = product(t_h, t_l, lift_t[...])
+        dx = (
+            wide[2 * L :]
+            + lroll(wide[L : L + R1], -LIFT_BACK)
+            + lroll(wide[:R1], -2 * LIFT_BACK)
+        )
         lane = lane_of(R)
         own = dx[L : L + R]
         lon = 0.5 * (dx[2 * L :] - dx[:R])
@@ -1055,7 +1089,14 @@
             x[:at_m], jnp.zeros((at_m, ch - L), f32)
         )
 
-    drain(jobs)
+    state_result = pltpu.make_async_copy(
+        all_out.at[all_rows:], final_out.at[all_rows:], out_sems.at[len(jobs)]
+    )
+    state_result.start()
+    drain(jobs[::-1])
+    state_result.wait()
+    for job in jobs:
+        job.result.wait()
 
 
 def hand_out(rows, weights, *outs):
@@ -1068,13 +1109,13 @@
         at += ref.shape[0]
     cin = lift.shape[2]
     vel = slice(3 * VARS, 5 * VARS)
-    for i in range(3):
-        for j in range(3):
-            at = (i * 3 + j) * ch
-            lift[i, j] = weights[at : at + cin]
-            for b in range(2):
-                at_conv = at + (b + 1) * 9 * ch
-                conv[b, i, j] = weights[at_conv : at_conv + ch]
+    conv_base, qkv_base, out_base, head_base = bases(cin)
+    for k in range(9):
+        at = k * tap_rows(cin)
+        lift[k // 3, k % 3] = weights[at : at + cin]
+        for b in range(2):
+            at = conv_base + (b * 9 + k) * ch
+            conv[b, k // 3, k % 3] = weights[at : at + ch]
     lift_bias[...] = weights[cin : cin + 1]
     head_bias[...] = weights[cin + 1 : cin + 2, vel]
     for b in range(2):
@@ -1082,10 +1123,10 @@
         shift[b : b + 1] = weights[at : at + 1]
         gain[b : b + 1] = weights[at + 1 : at + 2]
     for k in range(3):
-        at = (27 + k) * ch
+        at = qkv_base + k * ch
         qkv[:, k * ch : (k + 1) * ch] = weights[at : at + ch]
-    out[...] = weights[30 * ch : 31 * ch]
-    head[...] = weights[31 * ch : 32 * ch].T[vel]
+    out[...] = weights[out_base : out_base + ch]
+    head[...] = weights[head_base + vel.start : head_base + vel.stop]
 
 
 def on_device(
@@ -1117,10 +1158,11 @@
         return x[0].transpose(2, 1, 0).reshape(-1, L)
 
     S = SECTIONS
-    rows = 32 * ch
+    cin = lift_weight.shape[2]
+    rows = bases(cin)[-1] + HEAD_ROWS
     rows = -(-rows // (8 * nd)) * 8 * nd
     stage_count = len(factors(nl, 2)) + len(factors(nb, 4))
-    job_count = len(job_plan(rows, 8 * nd))
+    job_count = len(job_plan(rows, 8 * nd, lift_weight.shape[2]))
     vm = pltpu.VMEM
     dma = pltpu.SemaphoreType.DMA
     scratch = [
@@ -1155,7 +1197,8 @@
         vm((R2, ch), f32),
         vm((W // 2, 4 * L, 2 * HEADS * L), f32),
         vm((3, 9 * ch, 3 * ch), bf16),
-        vm((3, 9 * ch, 3 * ch), bf16),
+        vm((2, 9 * ch, 3 * ch), bf16),
+        vm((6 * ch, 2 * ch), bf16),
         vm((2 * ch, 6 * ch), bf16),
         vm((6 * ch, 2 * ch), bf16),
         vm((2 * ch, 2 * ch), bf16),
@@ -1186,6 +1229,8 @@
         vm((rows, ch), f32),
         vm((2, 2, ch), f32),
         vm((2, ch), f32),
+        vm((rows + 8 + 6 * VARS * W, ch), f32),
+        dma((job_count + 1,)),
         vm((32 * W, L), f32),
         vm((W, L), jnp.int32),
         vm((R, context.shape[-1]), f32),
@@ -1215,7 +1260,7 @@
         partial(kernel, (nl, nb, L, W, HEADS)),
         out_shape=jax.ShapeDtypeStruct((rows + 8 + 6 * VARS * W, ch), f32),
         in_specs=[apart] * 12 + [whole] * 4,
-        out_specs=whole,
+        out_specs=apart,
         scratch_shapes=scratch,
         compiler_params=pltpu.CompilerParams(
             collective_id=0, has_side_effects=True, vmem_limit_bytes=60 * 2**20

time: 165 us -> 162 us (0.982)
  Pallas kernels: 163 us -> 159 us
    pallas_call x1, Pallas kernels: 161 us -> 158 us  [on_device(): pl.pallas_call(partial(kernel, (nl, nb, L, W, HEADS)), out_shape=jax.Shap...]
where the time goes in v5:
time: 162 us
  Pallas kernels  159 us (98%)
  local copies, waits for them, and re-layouts  1.62 us (1%)
    pallas_call x1, Pallas kernels, on_device(): pl.pallas_call(partial(kernel, (nl, nb, L, W, HEADS)), out_shape=jax.Shap...  158 us

profile of v5, /device:TPU:0, one launch (start us, length us, event | category | flops | bytes accessed | tf_op | source)
XLA Modules:
  0.0 161.7 jit_solution(10694162215944445415)
XLA Ops:
  0.7 158.0 %shard_map.255.weights = f32[4328,128]{1,0:T(8,128)} custom-call(f32[80,32]{1,0:T(8,128)} %bitcast.55, f32[160,32]{1,0:T(8,128)} %bitcast.52, f32[80,32]{1,0:T(8,128)} %bitcast.56, f32[160,32]{1,0:T(8,128)} %bitcast.53, s32[16,32]{1,0:T(8,128)} %bitcast.57, f32[512,75]{1,0:T(8,128)} %bitcast.51, s32[16,8,32]{2,1,0:T(8,128)} %bitcast.54, ...), custom_call_target="tpu_custom_call" | custom-call | tf_op jit(solution)/shard_map/pallas_call | solution.py:1259
  158.6 0.0 copy-start
  158.6 1.6 copy-done
  160.3 1.5 shard_map.256
Async XLA Ops:
  158.6 1.6 %copy-start = (f32[4328,128]{1,0:T(8,128)S(1)}, f32[4328,128]{1,0:T(8,128)}, u32[]{:S(2)}) copy-start(f32[4328,128]{1,0:T(8,128)} %shard_map.255.weights) | copy-start | bytes 6647812

commit v6 on v5

--- a/solution.py
+++ b/solution.py
@@ -143,6 +143,9 @@
     tl,
     lift_th,
     lift_tl,
+    flux_parts,
+    flux_velocity,
+    lift_sums,
     dqkv,
     dh2,
     h2,
@@ -572,6 +575,45 @@
                     at = (p * 3 + i) * ch
                     w3t[b - 1, at : at + ch, j * ch : (j + 1) * ch] = part
 
+    pair = 2 * L
+    last = W // 2 - 1
+    all_own = [(0, R)]
+    own_edges, own_inner = [(0, pair), (R - pair, R)], [(pair, R - pair)]
+    lift_bias = lift_bias_ref[...]
+
+    def stats(h, ranges):
+        weighted = h * rows_of(mask, ranges, 2 * L)
+        return jnp.concatenate(
+            [
+                jnp.sum(weighted, axis=0, keepdims=True),
+                jnp.sum(weighted * h, axis=0, keepdims=True),
+            ],
+            axis=0,
+        )
+
+    def lift(s, ranges):
+        value = conv(xh.at[s], xl.at[s], ranges, w3f[0]) + lift_bias
+        put_rows(h0.at[s], value, ranges, 2 * L)
+        return stats(value, ranges)
+
+    def lay(s, a, b):
+        y = ys[s, L + a : L + b]
+        lane = lane_of(b - a)
+        lon = 0.5 * (ys[s, 2 * L + a : 2 * L + b] - ys[s, a:b])
+        x = jnp.where(
+            (lane >= VARS) & (lane < 2 * VARS),
+            lat_diff(y),
+            jnp.where((lane >= 2 * VARS) & (lane < 3 * VARS), lon, y),
+        )
+        hi, lo = split(x)
+        xh[s, a:b] = hi
+        xl[s, a:b] = lo
+
+    def lift_inner(s):
+        lay(s, pair, R1 - pair)
+        lift_sums[...] = lift(s, own_inner)
+
+    lift_inner(0)
     pl.semaphore_wait(barrier, nd - 1)
     halo_start(0, ys, 0, 2)
     sum_start(4 * SECTIONS, jnp.concatenate([count_part, count_part], axis=0))
@@ -605,11 +647,11 @@
         gk[s] = cot * (weight * step_size / 6.0)
     grad_ref[...] = cot
     acc[...] = jnp.zeros_like(acc)
+    dqkv[...] = jnp.zeros_like(dqkv)
     gw[...] = jnp.zeros_like(gw)
     norm_acc[...] = jnp.zeros_like(norm_acc)
     bias_acc[...] = jnp.zeros_like(bias_acc)
 
-    pair = 2 * L
     shape = (2 * pair, HEADS * pair)
     key_of = lax.broadcasted_iota(jnp.int32, shape, 0)
     key_of = key_of - lax.broadcasted_iota(jnp.int32, shape, 1) // L % 2 * L
@@ -635,20 +677,9 @@
         x = x * head_mask
         return sum(x[h * pair : (h + 1) * pair] for h in range(1, HEADS)) + x[:pair]
 
-    lift_bias = lift_bias_ref[...]
     head_bias = head_bias_row[...]
     gains = [gain_ref[0:1], gain_ref[1:2]]
     shifts = [shift_ref[0:1], shift_ref[1:2]]
-
-    def stats(h, ranges):
-        weighted = h * rows_of(mask, ranges, 2 * L)
-        return jnp.concatenate(
-            [
-                jnp.sum(weighted, axis=0, keepdims=True),
-                jnp.sum(weighted * h, axis=0, keepdims=True),
-            ],
-            axis=0,
-        )
 
     def normalise(s, b, sums):
         total_count = count[0:1]
@@ -667,38 +698,15 @@
         )
         return z * below, slope
 
-    last = W // 2 - 1
-    all_own = [(0, R)]
-    own_edges, own_inner = [(0, pair), (R - pair, R)], [(pair, R - pair)]
 
     def forward(s, carry):
         hb = s * 6
         ext = 2 * pair
 
-        def lift(ranges):
-            value = conv(xh.at[s], xl.at[s], ranges, w3f[0]) + lift_bias
-            put_rows(h0.at[s], value, ranges, 2 * L)
-            return stats(value, ranges)
-
-        def lay(a, b):
-            y = ys[s, L + a : L + b]
-            lane = lane_of(b - a)
-            lon = 0.5 * (ys[s, 2 * L + a : 2 * L + b] - ys[s, a:b])
-            x = jnp.where(
-                (lane >= VARS) & (lane < 2 * VARS),
-                lat_diff(y),
-                jnp.where((lane >= 2 * VARS) & (lane < 3 * VARS), lon, y),
-            )
-            hi, lo = split(x)
-            xh[s, a:b] = hi
-            xl[s, a:b] = lo
-
-        lay(pair, R1 - pair)
-        sums = lift(own_inner)
         halo_wait(hb, ys, s, 2)
-        lay(0, pair)
-        lay(R1 - pair, R1)
-        sum_start(s * 4, sums + lift(own_edges))
+        lay(s, 0, pair)
+        lay(s, R1 - pair, R1)
+        sum_start(s * 4, lift_sums[...] + lift(s, own_edges))
         halo_start(hb + 1, h0, s, 2)
         y1 = ys[s, L : L + R1]
         lane = lane_of(R1)
@@ -825,6 +833,7 @@
         second_block([(ext, R1 - ext)])
         attend(range(1, last))
         finish(own_inner)
+        pl.when(s < SECTIONS - 1)(lambda: lift_inner(s + 1))
         return carry
 
     lax.fori_loop(0, SECTIONS, forward, 0)
@@ -859,7 +868,6 @@
         g_h, g_l = split(gk[s])
         gh[...] = g_h
         gl[...] = g_l
-        dqkv[...] = jnp.zeros_like(dqkv)
 
         def head_back(ranges):
             hi, lo = rows_of(gh, ranges), rows_of(gl, ranges)
@@ -945,6 +953,9 @@
         bias_acc[1:2] += jnp.sum(gk[s], axis=0, keepdims=True)
         part = rows_product(gh[...], gl[...], h3h[s], h3l[s])
         gw[head_base : head_base + HEAD_ROWS] += part[:HEAD_ROWS]
+        gw[out_base : out_base + ch] += rows_product(
+            bh[s], bl[s], dh3h[...], dh3l[...]
+        )
         for e in edges:
             e.wait()
         dh2[:pair] += rb[s, 1, :pair]
@@ -959,9 +970,6 @@
         sum_start(s * 4 + 2, sums)
         de1[s, 2 * L : 2 * L + R] = direct
         halo_start(hb + 4, de1, s, 1)
-        gw[out_base : out_base + ch] += rows_product(
-            bh[s], bl[s], dh3h[...], dh3l[...]
-        )
         d_h, d_l = split(dqkv[...])
         wide = rows_product(h2h[s], h2l[s], d_h, d_l)
         for k in range(3):
@@ -999,6 +1007,19 @@
             )
 
         pl.when(s < SECTIONS - 1)(lambda: lift_grad(s + 1))
+        dqkv[...] = jnp.zeros_like(dqkv)
+        lane = lane_of(R)
+        g = gk[s]
+        g_lon = jnp.concatenate([g[L:], rb[s, 0, pair:]], axis=0)
+        g_lon = 0.5 * (
+            g_lon - jnp.concatenate([rb[s, 1, pair:], g[: R - L]], axis=0)
+        )
+        dflux = jnp.where(
+            lane < VARS, lat_diff(g), jnp.where(lane < 2 * VARS, g_lon, 0.0)
+        )
+        y = ys[s, 2 * L : 2 * L + R]
+        flux_parts[...] = dflux * lroll(y, -3 * VARS)
+        flux_velocity[...] = lroll(dflux * y, 3 * VARS)
         pl.when(s == 0)(lambda: advance(2))
         sums = sum_wait(s * 4 + 3)
         halo_wait(hb + 5, de0, s, 2)
@@ -1028,21 +1049,12 @@
         lane = lane_of(R)
         own = dx[L : L + R]
         lon = 0.5 * (dx[2 * L :] - dx[:R])
-        g = gk[s]
-        g_lon = jnp.concatenate([g[L:], rb[s, 0, 2 * L :]], axis=0)
-        g_lon = 0.5 * (
-            g_lon - jnp.concatenate([rb[s, 1, 2 * L :], g[: R - L]], axis=0)
-        )
-        dflux = jnp.where(
-            lane < VARS, lat_diff(g), jnp.where(lane < 2 * VARS, g_lon, 0.0)
-        )
-        y = ys[s, 2 * L : 2 * L + R]
         parts = jnp.where(
             lane < VARS,
             own,
             jnp.where(lane < 2 * VARS, -lat_diff(own), -lon),
         )
-        parts = parts + dflux * lroll(y, -3 * VARS)
+        parts = parts + flux_parts[...]
         parts = jnp.where(lane < 3 * VARS, parts, 0.0)
         fields_grad = (
             parts
@@ -1051,7 +1063,7 @@
             + lroll(parts, -VARS)
             + lroll(parts, -2 * VARS)
         )
-        velocity_grad = own + lroll(dflux * y, 3 * VARS)
+        velocity_grad = own + flux_velocity[...]
         gy = jnp.where(
             lane < 3 * VARS,
             fields_grad,
@@ -1217,6 +1229,9 @@
         vm((R1, 3 * ch), bf16),
         vm((R, 3 * ch), bf16),
         vm((R, 3 * ch), bf16),
+        vm((R, ch), f32),
+        vm((R, ch), f32),
+        vm((2, ch), f32),
         vm((R1, 3 * ch), f32),
         vm((R1, ch), f32),
         vm((R1, ch), f32),

time: 162 us -> 161 us (level)
  no operation moved by 1% of the time
where the time goes in v6:
time: 161 us
  Pallas kernels  159 us (99%)
  local copies, waits for them, and re-layouts  1.62 us (1%)
    pallas_call x1, Pallas kernels, on_device(): pl.pallas_call(partial(kernel, (nl, nb, L, W, HEADS)), out_shape=jax.Shap...  157 us

profile of v6, /device:TPU:0, one launch (start us, length us, event | category | flops | bytes accessed | tf_op | source)
XLA Modules:
  0.0 161.1 jit_solution(1784325497714163408)
XLA Ops:
  0.7 157.3 %shard_map.255.weights = f32[4328,128]{1,0:T(8,128)} custom-call(f32[80,32]{1,0:T(8,128)} %bitcast.55, f32[160,32]{1,0:T(8,128)} %bitcast.52, f32[80,32]{1,0:T(8,128)} %bitcast.56, f32[160,32]{1,0:T(8,128)} %bitcast.53, s32[16,32]{1,0:T(8,128)} %bitcast.57, f32[512,75]{1,0:T(8,128)} %bitcast.51, s32[16,8,32]{2,1,0:T(8,128)} %bitcast.54, ...), custom_call_target="tpu_custom_call" | custom-call | tf_op jit(solution)/shard_map/pallas_call | solution.py:1274
  158.0 0.0 copy-start
  158.0 1.6 %copy-done = f32[4328,128]{1,0:T(8,128)S(1)} copy-done((f32[4328,128]{1,0:T(8,128)S(1)}, f32[4328,128]{1,0:T(8,128)}, u32[]{:S(2)}) %copy-start) | copy-done | bytes 2215960
  159.6 1.5 shard_map.256
Async XLA Ops:
  158.0 1.6 %copy-start = (f32[4328,128]{1,0:T(8,128)S(1)}, f32[4328,128]{1,0:T(8,128)}, u32[]{:S(2)}) copy-start(f32[4328,128]{1,0:T(8,128)} %shard_map.255.weights) | copy-start | bytes 6647812

commit v7 on v6

--- a/solution.py
+++ b/solution.py
@@ -951,11 +951,6 @@
         triple([(pair, R1 - pair)])
         (inner_act,) = conv_back(th, tl, own_inner, w3t[1])
         bias_acc[1:2] += jnp.sum(gk[s], axis=0, keepdims=True)
-        part = rows_product(gh[...], gl[...], h3h[s], h3l[s])
-        gw[head_base : head_base + HEAD_ROWS] += part[:HEAD_ROWS]
-        gw[out_base : out_base + ch] += rows_product(
-            bh[s], bl[s], dh3h[...], dh3l[...]
-        )
         for e in edges:
             e.wait()
         dh2[:pair] += rb[s, 1, :pair]
@@ -970,6 +965,11 @@
         sum_start(s * 4 + 2, sums)
         de1[s, 2 * L : 2 * L + R] = direct
         halo_start(hb + 4, de1, s, 1)
+        part = rows_product(gh[...], gl[...], h3h[s], h3l[s])
+        gw[head_base : head_base + HEAD_ROWS] += part[:HEAD_ROWS]
+        gw[out_base : out_base + ch] += rows_product(
+            bh[s], bl[s], dh3h[...], dh3l[...]
+        )
         d_h, d_l = split(dqkv[...])
         wide = rows_product(h2h[s], h2l[s], d_h, d_l)
         for k in range(3):
@@ -1111,34 +1111,56 @@
         job.result.wait()
 
 
-def hand_out(rows, weights, *outs):
-    fields = outs[:4]
-    lift, lift_bias, gain, shift, conv, qkv, out, head, head_bias = outs[4:]
+def hand_out(rows, cin, results, *refs):
+    fields = refs[:4]
+    lift, lift_bias, gain, shift, conv, qkv, out, head, head_bias = refs[4:13]
+    weights, sems = refs[13:]
     ch = LANES
-    at = rows + 8
-    for ref in fields:
-        ref[...] = weights[at : at + ref.shape[0], : ref.shape[1]]
-        at += ref.shape[0]
-    cin = lift.shape[2]
     vel = slice(3 * VARS, 5 * VARS)
     conv_base, qkv_base, out_base, head_base = bases(cin)
+
+    def load(k, a, b):
+        copy = pltpu.make_async_copy(results.at[a:b], weights.at[a:b], sems.at[k])
+        copy.start()
+        return copy
+
+    half = conv_base + (qkv_base - conv_base) // 2
+    conv_parts = [load(1, conv_base, half), load(2, half, qkv_base)]
+    lift_part = load(0, 0, conv_base)
+    rest = load(3, qkv_base, weights.shape[0])
+    backs = []
+    for k, (part, a, b) in enumerate(
+        zip(conv_parts, (conv_base, half), (half, qkv_base))
+    ):
+        part.wait()
+        backs.append(
+            pltpu.make_async_copy(
+                weights.at[a:b], conv.at[a - conv_base : b - conv_base], sems.at[4 + k]
+            )
+        )
+        backs[-1].start()
+    lift_part.wait()
     for k in range(9):
         at = k * tap_rows(cin)
         lift[k // 3, k % 3] = weights[at : at + cin]
-        for b in range(2):
-            at = conv_base + (b * 9 + k) * ch
-            conv[b, k // 3, k % 3] = weights[at : at + ch]
     lift_bias[...] = weights[cin : cin + 1]
     head_bias[...] = weights[cin + 1 : cin + 2, vel]
-    for b in range(2):
-        at = rows + 2 * b
-        shift[b : b + 1] = weights[at : at + 1]
-        gain[b : b + 1] = weights[at + 1 : at + 2]
+    rest.wait()
     for k in range(3):
         at = qkv_base + k * ch
         qkv[:, k * ch : (k + 1) * ch] = weights[at : at + ch]
     out[...] = weights[out_base : out_base + ch]
     head[...] = weights[head_base + vel.start : head_base + vel.stop]
+    for b in range(2):
+        at = rows + 2 * b
+        shift[b : b + 1] = weights[at : at + 1]
+        gain[b : b + 1] = weights[at + 1 : at + 2]
+    at = rows + 8
+    for ref in fields:
+        ref[...] = weights[at : at + ref.shape[0], : ref.shape[1]]
+        at += ref.shape[0]
+    for copy in backs:
+        copy.wait()
 
 
 def on_device(
@@ -1308,18 +1330,19 @@
         (1, ch),
         norm_gain.shape,
         norm_shift.shape,
-        conv_weight.shape,
+        (18 * ch, ch),
         attn_qkv.shape,
         attn_out.shape,
         head_weight.shape[::-1],
         (1, head_bias.shape[0]),
     )
     outs = pl.pallas_call(
-        partial(hand_out, rows),
+        partial(hand_out, rows, cin),
         out_shape=tuple(jax.ShapeDtypeStruct(shape, f32) for shape in shapes),
-        in_specs=[whole],
-        out_specs=(whole,) * len(shapes),
-        compiler_params=pltpu.CompilerParams(vmem_limit_bytes=32 * 2**20),
+        in_specs=[apart],
+        out_specs=tuple(apart if k == 8 else whole for k in range(13)),
+        scratch_shapes=[vm(results.shape, f32), dma((6,))],
+        compiler_params=pltpu.CompilerParams(vmem_limit_bytes=60 * 2**20),
     )(results)
 
     def field(x):
@@ -1329,7 +1352,9 @@
         *(field(x) for x in outs[:4]),
         outs[4],
         outs[5][0],
-        *outs[6:11],
+        *outs[6:8],
+        outs[8].reshape(conv_weight.shape),
+        *outs[9:11],
         outs[11].T,
         outs[12][0],
     )

time: 161 us -> 161 us (level)
  local copies, waits for them, and re-layouts: 1.62 us -> 0 us
    pallas_call x1, Pallas kernels: 1.46 us -> 3.08 us  [on_device(): pl.pallas_call(partial(hand_out, rows, cin), out_shape=tuple((jax.ShapeDt...]
    unnamed x2 -> x0, local copies, waits for them, and re-layouts: 1.62 us -> none
where the time goes in v7:
time: 161 us; the launch traced here: 160 us
  Pallas kernels  160 us (99%)
    pallas_call x1, Pallas kernels, on_device(): pl.pallas_call(partial(kernel, (nl, nb, L, W, HEADS)), out_shape=jax.Shap...  156 us

profile of v7, /device:TPU:0, one launch (start us, length us, event | category | flops | bytes accessed | tf_op | source)
XLA Modules:
  0.0 160.4 jit_solution(14678637783434315550)
XLA Ops:
  0.7 156.5 %shard_map.255.results = f32[4328,128]{1,0:T(8,128)} custom-call(f32[80,32]{1,0:T(8,128)} %bitcast.56, f32[160,32]{1,0:T(8,128)} %bitcast.53, f32[80,32]{1,0:T(8,128)} %bitcast.57, f32[160,32]{1,0:T(8,128)} %bitcast.54, s32[16,32]{1,0:T(8,128)} %bitcast.58, f32[512,75]{1,0:T(8,128)} %bitcast.52, s32[16,8,32]{2,1,0:T(8,128)} %bitcast.55, ...), custom_call_target="tpu_custom_call" | custom-call | tf_op jit(solution)/shard_map/pallas_call | solution.py:1296
  157.1 3.1 %shard_map.256 = (f32[80,32]{1,0:T(8,128)}, f32[160,32]{1,0:T(8,128)}, f32[80,32]{1,0:T(8,128)}, f32[160,32]{1,0:T(8,128)}, f32[3,3,100,128]{3,2,1,0:T(8,128)}, ...) custom-call(f32[4328,128]{1,0:T(8,128)} %shard_map.255.results), custom_call_target="tpu_custom_call" | custom-call | tf_op jit(solution)/shard_map/pallas_call | solution.py:1339
